TPU v7x, 32 devices: a whole 2x2x4 slice. The times are simulated.
32 devices in a mesh: sup: 2 (over y), row: 8 (over z, x), col: 2 (over core).
Axes of the slice: x: 2, y: 2, z: 4, core: 2. Of those that a mesh axis runs over, the one named last changes fastest.
Arguments:
- schur_block: float32 [24576, 12288], P(('sup', 'row'), 'col'), parts along dimension 0, may hold values from -6 to 6
- w_first: bfloat16 [80, 12288], P(('sup', 'row'), 'col'), parts along dimension 0, may hold values from -2 to 2
- w_second: bfloat16 [80, 12288], P(('sup', 'row'), 'col'), parts along dimension 0, may hold values from -2 to 2
Outputs:
- condensed: float32 [24576, 12288], P(('sup', 'row'), 'col'), parts along dimension 0
There are 2 independent parts, one for each index of `sup`. A program takes and returns all parts, laid end to end along the dimension named above; each array names one. Nothing has to cross between parts.
All inputs are finite; a program needn't handle non-finite values.
Results may differ from a plain program's by a relative error of at most 0.0003.
Values may be sent and summed in bfloat16 or wider, within the bound.
No kernel may reach another device: no remote copies, remote signals or barrier semaphores. Data moves between devices by JAX's collectives and lax.ppermute only.
A program may use at most 192 MiB of HBM per device.

v0:
```python
import jax
import jax.numpy as jnp
from jax import lax
from jax.sharding import PartitionSpec as P


def from_partner(block, axis, bit):
    count = lax.axis_size(axis)
    route = []
    for low in range(count):
        high = low | 1 << bit
        if high != low and high < count:
            route += [(low, high), (high, low)]
    return lax.ppermute(block, axis, route)


def contract_rows(left_part, right_part):
    return lax.dot_general(
        left_part, right_part, (((0,), (0,)), ((), ())), preferred_element_type=jnp.float32
    )


def per_device(schur_block, w_first, w_second):
    row_count = lax.axis_size("row")
    col_count = lax.axis_size("col")
    tile_rows = schur_block.shape[0]
    row_index = lax.axis_index("row")
    col_index = lax.axis_index("col")
    local_rows = w_first.shape[0]
    per_column = row_count // col_count

    def outgoing(slab):
        blocks = jnp.transpose(slab.reshape(local_rows, per_column, tile_rows), (1, 0, 2))
        return jnp.concatenate([blocks] * col_count, axis=0)

    got_first, got_second = (
        lax.all_to_all(outgoing(w_first), "row", split_axis=0, concat_axis=0, tiled=True),
        lax.all_to_all(outgoing(w_second), "row", split_axis=0, concat_axis=0, tiled=True),
    )
    own_first = got_first.reshape(row_count * local_rows, tile_rows)
    own_second = got_second.reshape(row_count * local_rows, tile_rows)
    peer_first, peer_second = from_partner((own_first, own_second), "col", 0)
    owner_side = col_index == row_index // per_column
    left_first = jnp.where(owner_side, own_first, peer_first)
    left_second = jnp.where(owner_side, own_second, peer_second)
    update = contract_rows(
        left_first, lax.all_gather(w_first, "row", axis=0, tiled=True)
    ) + contract_rows(left_second, lax.all_gather(w_second, "row", axis=0, tiled=True))
    return schur_block - update


def solution(mesh):
    placed = (P(("sup", "row"), "col"), P(("sup", "row"), "col"), P(("sup", "row"), "col"))
    return jax.shard_map(
        per_device, mesh=mesh, in_specs=placed, out_specs=P(("sup", "row"), "col"), check_vma=False
    )
```

profile of v0, /device:TPU:1, one launch (start us, length us, event | category | flops | bytes accessed | tf_op | source)
XLA Modules:
  0.0 137.4 jit_solution(17893648522282628936)
XLA Ops:
  0.0 1.7 %pad_maximum_fusion.1 = bf16[8,5,1536]{2,1,0:T(8,128)(2,1)} fusion(bf16[4,5,1536]{2,1,0:T(8,128)(2,1)} %bitcast.10), kind=kLoop, calls=%fused_computation.2 | loop fusion | flops 61440 | bytes 184320 | tf_op jit(solution)/shard_map/concatenate | solution.py:34
  1.7 6.4 %all-to-all-start.1 = ((bf16[8,5,1536]{2,1,0:T(8,128)(2,1)}), bf16[8,5,1536]{2,1,0:T(8,128)(2,1)S(1)}, u32[]{:S(2)}, u32[]{:S(2)}) async-start(bf16[8,5,1536]{2,1,0:T(8,128)(2,1)} %pad_maximum_fusion.1), calls=%async_computation.1 | async-start | bytes 393216 | tf_op jit(solution)/shard_map/all_to_all | solution.py:38
  8.0 27.9 %all-gather.1 = bf16[8,5,6144]{2,1,0:T(8,128)(2,1)S(1)} all-gather(bf16[1,5,6144]{2,1,0:T(8,128)(2,1)} %bitcast.11), channel_id=1, replica_groups=mesh['sup'=2,'row'=8,'col'=2] {'row'}, dimensions={0}, use_global_device_ids=true | all-gather | bytes 552960 | tf_op jit(solution)/shard_map/all_gather | solution.py:48
  35.9 0.2 reshape.19
  36.1 1.7 %pad_maximum_fusion = bf16[8,5,1536]{2,1,0:T(8,128)(2,1)} fusion(bf16[4,5,1536]{2,1,0:T(8,128)(2,1)} %bitcast.12), kind=kLoop, calls=%fused_computation.1 | loop fusion | flops 61440 | bytes 184320 | tf_op jit(solution)/shard_map/concatenate | solution.py:34
  37.8 0.0 all-to-all-done.1
  37.8 3.9 %all-to-all-start = ((bf16[8,5,1536]{2,1,0:T(8,128)(2,1)}), bf16[8,5,1536]{2,1,0:T(8,128)(2,1)S(1)}, u32[]{:S(2)}, u32[]{:S(2)}) async-start(bf16[8,5,1536]{2,1,0:T(8,128)(2,1)} %pad_maximum_fusion), calls=%async_computation | async-start | bytes 393216 | tf_op jit(solution)/shard_map/all_to_all | solution.py:37
  41.7 0.1 reshape.15
  41.8 7.7 %collective-permute-start.1 = (bf16[40,1536]{1,0:T(8,128)(2,1)S(1)}, bf16[40,1536]{1,0:T(8,128)(2,1)S(1)}, u32[]{:S(2)}, u32[]{:S(2)}) collective-permute-start(bf16[40,1536]{1,0:T(8,128)(2,1)S(1)} %reshape.15), channel_id=1, source_target_pairs={{0,1},{1,0},{2,3},{3,2},{4,5},{5,4},{6,7},{7,6},{8,9},{9,8},{10,11... | collective-permute-start | bytes 368648 | tf_op jit(solution)/shard_map/ppermute | solution.py:14
  49.5 27.8 %all-gather = bf16[8,5,6144]{2,1,0:T(8,128)(2,1)S(1)} all-gather(bf16[1,5,6144]{2,1,0:T(8,128)(2,1)} %bitcast.13), channel_id=1, replica_groups=mesh['sup'=2,'row'=8,'col'=2] {'row'}, dimensions={0}, use_global_device_ids=true | all-gather | bytes 552960 | tf_op jit(solution)/shard_map/all_gather | solution.py:47
  77.3 0.2 reshape.17
  77.5 0.0 all-to-all-done
  77.5 0.1 reshape.13
  77.6 5.9 %collective-permute-start = (bf16[40,1536]{1,0:T(8,128)(2,1)S(1)}, bf16[40,1536]{1,0:T(8,128)(2,1)S(1)}, u32[]{:S(2)}, u32[]{:S(2)}) collective-permute-start(bf16[40,1536]{1,0:T(8,128)(2,1)S(1)} %reshape.13), channel_id=1, source_target_pairs={{0,1},{1,0},{2,3},{3,2},{4,5},{5,4},{6,7},{7,6},{8,9},{9,8},{10,11... | collective-permute-start | bytes 368648 | tf_op jit(solution)/shard_map/ppermute | solution.py:14
  83.5 0.0 collective-permute-done.1
  83.5 15.7 %fusion = f32[1536,6144]{1,0:T(8,128)} fusion(bf16[40,6144]{1,0:T(8,128)(2,1)S(1)} %reshape.19, bf16[40,1536]{1,0:T(8,128)(2,1)S(1)} %reshape.15, bf16[40,1536]{1,0:T(8,128)(2,1)S(1)} %collective-permute-done.1, pred[]{:T(512)S(6)} %eq.3), kind=kOutput, calls=%fused_computation.3 | convolution fusion | flops 755036160 | bytes 38486016 | tf_op jit(solution)/shard_map/dot_general | solution.py:18
  99.2 0.0 collective-permute-done
  99.2 38.1 %add_subtract_fusion = f32[1536,6144]{1,0:T(8,128)} fusion(f32[1536,6144]{1,0:T(8,128)} %param.3, f32[1536,6144]{1,0:T(8,128)} %fusion, bf16[40,6144]{1,0:T(8,128)(2,1)S(1)} %reshape.17, bf16[40,1536]{1,0:T(8,128)(2,1)S(1)} %reshape.13, bf16[40,1536]{1,0:T(8,128)(2,1)S(1)} %collective-permute-done, pred[]{:T(512)S(6)} %eq.3), kind=kOutput, calls=%fused_computation | convolution fusion | flops 773910528 | bytes 113983488 | tf_op jit(solution)/shard_map/dot_general | solution.py:18
Async XLA Ops:
  1.7 36.1 %all-to-all-start.1 = ((bf16[8,5,1536]{2,1,0:T(8,128)(2,1)}), bf16[8,5,1536]{2,1,0:T(8,128)(2,1)S(1)}, u32[]{:S(2)}, u32[]{:S(2)}) async-start(bf16[8,5,1536]{2,1,0:T(8,128)(2,1)} %pad_maximum_fusion.1), calls=%async_computation.1 | async-start | bytes 393216 | tf_op jit(solution)/shard_map/all_to_all | solution.py:38
  37.8 39.7 %all-to-all-start = ((bf16[8,5,1536]{2,1,0:T(8,128)(2,1)}), bf16[8,5,1536]{2,1,0:T(8,128)(2,1)S(1)}, u32[]{:S(2)}, u32[]{:S(2)}) async-start(bf16[8,5,1536]{2,1,0:T(8,128)(2,1)} %pad_maximum_fusion), calls=%async_computation | async-start | bytes 393216 | tf_op jit(solution)/shard_map/all_to_all | solution.py:37
  41.8 41.7 %collective-permute-start.1 = (bf16[40,1536]{1,0:T(8,128)(2,1)S(1)}, bf16[40,1536]{1,0:T(8,128)(2,1)S(1)}, u32[]{:S(2)}, u32[]{:S(2)}) collective-permute-start(bf16[40,1536]{1,0:T(8,128)(2,1)S(1)} %reshape.15), channel_id=1, source_target_pairs={{0,1},{1,0},{2,3},{3,2},{4,5},{5,4},{6,7},{7,6},{8,9},{9,8},{10,11... | collective-permute-start | bytes 368648 | tf_op jit(solution)/shard_map/ppermute | solution.py:14
  77.6 21.6 %collective-permute-start = (bf16[40,1536]{1,0:T(8,128)(2,1)S(1)}, bf16[40,1536]{1,0:T(8,128)(2,1)S(1)}, u32[]{:S(2)}, u32[]{:S(2)}) collective-permute-start(bf16[40,1536]{1,0:T(8,128)(2,1)S(1)} %reshape.13), channel_id=1, source_target_pairs={{0,1},{1,0},{2,3},{3,2},{4,5},{5,4},{6,7},{7,6},{8,9},{9,8},{10,11... | collective-permute-start | bytes 368648 | tf_op jit(solution)/shard_map/ppermute | solution.py:14
where the time goes:
time: 138 us; the launch traced here: 137 us
  blocking collectives  55.7 us (40%)
  matrix products  53.8 us (39%)
  starting transfers between devices  23.9 us (17%)
  other arithmetic  3.37 us (2%)
    dot_general x2, matrix products, contract_rows(): lax.dot_general(left_part, right_part, (((0,), (0,)), ((), ())), preferre...  53.8 us
    all_gather x1, blocking collectives, per_device(): lax.all_gather(w_second, 'row', axis=0, tiled=True)  27.9 us
    all_gather x1, blocking collectives, per_device(): lax.all_gather(w_first, 'row', axis=0, tiled=True)  27.8 us
    ppermute x2, starting transfers between devices, from_partner(): return lax.ppermute(block, axis, route)  13.6 us
    all_to_all x1, starting transfers between devices, per_device(): lax.all_to_all(outgoing(w_second), 'row', split_axis=0, concat_axis=0, ti...  6.35 us
    all_to_all x1, starting transfers between devices, per_device(): lax.all_to_all(outgoing(w_first), 'row', split_axis=0, concat_axis=0, til...  3.91 us
    concatenate x2, other arithmetic, outgoing(): return jnp.concatenate([blocks] * col_count, axis=0)  3.37 us
  transfers between devices with their start and end apart: 4, of which 0 were waited for; matrix products, arithmetic and copies ran while one was open for 13% of the time, Pallas kernels for 0%

commit v1 on v0

v1 whole, which is shorter than its diff:
```python
import functools

import jax
import jax.numpy as jnp
from jax import lax
from jax.experimental import pallas as pl
from jax.experimental.pallas import tpu as pltpu
from jax.sharding import PartitionSpec as P

MIB = 1 << 20
WHOLE = pl.BlockSpec(memory_space=pltpu.VMEM)


def in_vmem(array):
    return pltpu.with_memory_space_constraint(array, pltpu.VMEM)


class Packing:
    def __init__(self, rows, width):
        self.rows, self.width = rows, width
        self.full = rows // 8 * 8
        self.rest = rows - self.full
        self.fold = 8 // self.rest if self.rest else 1
        assert self.rest == 0 or (8 % self.rest == 0 and self.full == 8)
        assert width % (128 * self.fold) == 0
        self.chunk = width // self.fold
        self.packed = (self.full, width + (self.chunk if self.rest else 0))


def pack_kernel(packing, first_ref, second_ref, out_ref):
    local = first_ref.shape[0]
    both = jnp.concatenate([first_ref[...], second_ref[...]], axis=0)
    out_ref[:, : packing.width] = both[: packing.full]
    for i in range(packing.fold if packing.rest else 0):
        lanes = slice(i * packing.chunk, (i + 1) * packing.chunk)
        out_ref[i * packing.rest : (i + 1) * packing.rest, packing.width :] = both[packing.full :, lanes]


def pack(packing, first, second):
    return pl.pallas_call(
        functools.partial(pack_kernel, packing),
        in_specs=[WHOLE] * 2,
        out_specs=WHOLE,
        out_shape=jax.ShapeDtypeStruct(packing.packed, first.dtype),
        compiler_params=pltpu.CompilerParams(vmem_limit_bytes=8 * MIB),
        name="pack",
    )(first, second)


def gather_rows(block, axis):
    count = lax.axis_size(axis)
    if count > 16 or count % 2:
        return [lax.all_gather(block, axis, axis=0)]
    ring = [2 * i for i in range(count // 2)] + [2 * i + 1 for i in reversed(range(count // 2))]
    place = {index: position for position, index in enumerate(ring)}

    def step(array, by):
        return lax.ppermute(array, axis, [(i, ring[(place[i] + by) % count]) for i in range(count)])

    blocks, ahead, behind = [block], block, block
    for hop in range(1, count // 2 + 1):
        ahead = step(ahead, 1)
        blocks.append(ahead)
        if hop < (count + 1) // 2:
            behind = step(behind, -1)
            blocks.append(behind)
    return [b[None] for b in blocks]


def assemble_kernel(packing, tile, per_column, *refs):
    *piece_refs, right_ref, left_ref = refs
    count = sum(ref.shape[0] for ref in piece_refs)
    at = 0
    for ref in piece_refs:
        for p in range(ref.shape[0]):
            right_ref[at * packing.full : (at + 1) * packing.full, :] = ref[p, :, : packing.width]
            for i in range(packing.fold if packing.rest else 0):
                lanes = slice(i * packing.chunk, (i + 1) * packing.chunk)
                low = count * packing.full + at * packing.rest
                right_ref[low : low + packing.rest, lanes] = ref[
                    p, i * packing.rest : (i + 1) * packing.rest, packing.width :
                ]
            at += 1
    start = pl.multiple_of(lax.axis_index("row") % per_column * tile, 128)
    left_ref[...] = right_ref[:, pl.ds(start, tile)]


def assemble(packing, pieces, tile, per_column):
    depth = packing.rows * sum(p.shape[0] for p in pieces)
    dtype = pieces[0].dtype
    return pl.pallas_call(
        functools.partial(assemble_kernel, packing, tile, per_column),
        in_specs=[WHOLE] * len(pieces),
        out_specs=(WHOLE, WHOLE),
        out_shape=(pltpu.VMEM((depth, packing.width), dtype), pltpu.VMEM((depth, tile), dtype)),
        compiler_params=pltpu.CompilerParams(vmem_limit_bytes=16 * MIB),
        name="assemble",
    )(*[in_vmem(p) for p in pieces])


def assemble_plain(packing, pieces, tile, per_column):
    stack = jnp.concatenate(pieces, axis=0)
    count = stack.shape[0]
    top = stack[:, :, : packing.width].reshape(count * packing.full, packing.width)
    rest = stack[:, :, packing.width :].reshape(count, packing.fold, packing.rest, packing.chunk)
    rest = jnp.transpose(rest, (0, 2, 1, 3)).reshape(count * packing.rest, packing.width)
    right = jnp.concatenate([top, rest], axis=0)
    start = lax.axis_index("row") % per_column * tile
    return right, lax.dynamic_slice(right, (0, start), (right.shape[0], tile))


def update_kernel(block, slots, per_column, schur_ref, own_ref, peer_ref, right_ref, out_ref, left, right, stage, sems):
    rows, columns = block
    depth, width = right_ref.shape
    padded = right.shape[0]
    down, across = out_ref.shape[0] // rows, width // columns
    steps = down * across
    owner = lax.axis_index("col") == lax.axis_index("row") // per_column

    if padded > depth:
        left[:, depth:] = jnp.zeros((left.shape[0], padded - depth), left.dtype)
        right[depth:, :] = jnp.zeros((padded - depth, width), right.dtype)
    right[:depth, :] = right_ref[...]

    @pl.when(owner)
    def _():
        left[:, :depth] = own_ref[...].T

    @pl.when(jnp.logical_not(owner))
    def _():
        left[:, :depth] = peer_ref[...].T

    def place(t):
        i, j = t // across, t % across
        return pl.ds(pl.multiple_of(i * rows, rows), rows), pl.ds(pl.multiple_of(j * columns, columns), columns)

    def copy(t, slot):
        return pltpu.make_async_copy(stage.at[slot], out_ref.at[place(t)], sems.at[slot])

    def step(t, _):
        slot = t % slots

        @pl.when(t >= slots)
        def _():
            copy(t - slots, slot).wait()

        at_rows, at_columns = place(t)
        update = jnp.dot(left[at_rows, :], right[:, at_columns], preferred_element_type=jnp.float32)
        stage[slot] = schur_ref[at_rows, at_columns] - update
        copy(t, slot).start()
        return 0

    lax.fori_loop(0, steps, step, 0)
    for t in range(max(0, steps - slots), steps):
        copy(t, t % slots).wait()


def update(schur, own, peer, right, per_column):
    tile, width = schur.shape
    depth = right.shape[0]
    padded = -(-depth // 128) * 128
    rows = next(r for r in (512, 384, 256, 128, tile) if tile % r == 0)
    columns = next(c for c in (512, 384, 256, 128, width) if width % c == 0)
    slots = 6
    scratch = 4 * slots * rows * columns + 2 * padded * (tile + width)
    return pl.pallas_call(
        functools.partial(update_kernel, (rows, columns), slots, per_column),
        in_specs=[WHOLE] * 4,
        out_specs=pl.BlockSpec(memory_space=pl.ANY),
        out_shape=jax.ShapeDtypeStruct(schur.shape, schur.dtype),
        scratch_shapes=[
            pltpu.VMEM((tile, padded), right.dtype),
            pltpu.VMEM((padded, width), right.dtype),
            pltpu.VMEM((slots, rows, columns), jnp.float32),
            pltpu.SemaphoreType.DMA((slots,)),
        ],
        compiler_params=pltpu.CompilerParams(vmem_limit_bytes=scratch + 6 * MIB),
        name="update",
    )(in_vmem(schur), in_vmem(own), in_vmem(peer), in_vmem(right))


def per_device(schur_block, w_first, w_second):
    row_count = lax.axis_size("row")
    col_count = lax.axis_size("col")
    tile, width = schur_block.shape
    per_column = row_count // col_count
    packing = Packing(w_first.shape[0] + w_second.shape[0], width)
    pieces = gather_rows(pack(packing, w_first, w_second), "row")
    build = assemble if tile % 128 == 0 else assemble_plain
    right, own = build(packing, pieces, tile, per_column)
    peer = lax.ppermute(own, "col", [(c, (c + 1) % col_count) for c in range(col_count)])
    return update(schur_block, own, peer, right, per_column)


def solution(mesh):
    assert mesh.shape["col"] == 2
    placed = P(("sup", "row"), "col")
    return jax.shard_map(per_device, mesh=mesh, in_specs=(placed,) * 3, out_specs=placed, check_vma=False)
```

time: 138 us -> 49.8 us (0.36)
  blocking collectives: 55.7 us -> 0 us
  matrix products: 53.8 us -> 0 us
  starting transfers between devices: 23.9 us -> 10.7 us
  Pallas kernels: 0 us -> 13 us
  local copies, waits for them, and re-layouts: 0.56 us -> 13.5 us
  waiting for transfers between devices: 0.01 us -> 12 us
  other arithmetic: 3.37 us -> 0 us
    all_gather x2 -> x0, blocking collectives: 55.7 us -> none  [the longest x1 27.9 us: per_device(): lax.all_gather(w_second, 'row', axis=0, tiled=True)]
    dot_general x2 -> x0, matrix products: 53.8 us -> none  [contract_rows(): lax.dot_general(left_part, right_part, (((0,), (0,)), ((), ())), preferre...]
    unnamed x2 -> x6, local copies, waits for them, and re-layouts: 0.44 us -> 13.5 us
    pallas_call x0 -> x3, Pallas kernels: none -> 13 us  [the longest x1 12.8 us: update(): pl.pallas_call(functools.partial(update_kernel, (rows, columns), slots, p...]
    ppermute x2 -> x8, waiting for transfers between devices: 0.01 us -> 12 us  [the longest x7 10.9 us: step(): lax.ppermute(array, axis, [(i, ring[(place[i] + by) % count]) for i in ra...]
    all_to_all x2 -> x0, starting transfers between devices: 10.3 us -> none  [the longest x1 6.35 us: per_device(): lax.all_to_all(outgoing(w_second), 'row', split_axis=0, concat_axis=0, ti...]
    concatenate x2 -> x0, other arithmetic: 3.37 us -> none  [outgoing(): return jnp.concatenate([blocks] * col_count, axis=0)]
    ppermute x2 -> x8, starting transfers between devices: 13.6 us -> 10.7 us  [the longest x7 6.17 us: step(): lax.ppermute(array, axis, [(i, ring[(place[i] + by) % count]) for i in ra...]
  transfers between devices with their start and end apart: 4 -> 8, of which waited for: 0 -> 7; matrix products, arithmetic and copies ran while one was open for 13% -> 0% of each run, Pallas kernels for 0% -> 0%
where the time goes in v1:
time: 49.8 us; the launch traced here: 49.3 us
  local copies, waits for them, and re-layouts  13.5 us (27%)
  Pallas kernels  13 us (26%)
  waiting for transfers between devices  12 us (24%)
  starting transfers between devices  10.7 us (21%)
    unnamed x6, local copies, waits for them, and re-layouts  13.5 us
    pallas_call x1, Pallas kernels, update(): pl.pallas_call(functools.partial(update_kernel, (rows, columns), slots, p...  12.8 us
    ppermute x7, waiting for transfers between devices, step(): lax.ppermute(array, axis, [(i, ring[(place[i] + by) % count]) for i in ra...  10.9 us
    ppermute x7, starting transfers between devices, step(): lax.ppermute(array, axis, [(i, ring[(place[i] + by) % count]) for i in ra...  6.17 us
    ppermute x1, starting transfers between devices, per_device(): lax.ppermute(own, 'col', [(c, (c + 1) % col_count) for c in range(col_cou...  4.54 us
    ppermute x1, waiting for transfers between devices, per_device(): lax.ppermute(own, 'col', [(c, (c + 1) % col_count) for c in range(col_cou...  1.14 us
  transfers between devices with their start and end apart: 8, of which 7 were waited for; matrix products, arithmetic and copies ran while one was open for 0% of the time, Pallas kernels for 0%

profile of v1, /device:TPU:1, one launch (start us, length us, event | category | flops | bytes accessed | tf_op | source)
XLA Modules:
  0.0 49.3 jit_solution(17018256476644491447)
XLA Ops:
  0.0 0.0 copy-start.1
  0.0 0.9 %copy-done.1 = bf16[5,6144]{1,0:T(8,128)(2,1)S(1)} copy-done((bf16[5,6144]{1,0:T(8,128)(2,1)S(1)}, bf16[5,6144]{1,0:T(8,128)(2,1)}, u32[]{:S(2)}) %copy-start.1) | copy-done | bytes 61464
  0.9 0.0 copy-start.2
  0.9 0.9 %copy-done.2 = bf16[5,6144]{1,0:T(8,128)(2,1)S(1)} copy-done((bf16[5,6144]{1,0:T(8,128)(2,1)S(1)}, bf16[5,6144]{1,0:T(8,128)(2,1)}, u32[]{:S(2)}) %copy-start.2) | copy-done | bytes 61464
  1.8 0.1 pack.1
  1.9 2.2 %collective-permute-start = (bf16[8,7680]{1,0:T(8,128)(2,1)S(1)}, bf16[8,7680]{1,0:T(8,128)(2,1)S(1)}, u32[]{:S(2)}, u32[]{:S(2)}) collective-permute-start(bf16[8,7680]{1,0:T(8,128)(2,1)S(1)} %pack.1), channel_id=1, source_target_pairs={{0,4},{2,0},{4,8},{6,2},{8,12},{10,6},{12,14},{14,10},{1,5},{3,1},... | collective-permute-start | bytes 368648 | tf_op jit(solution)/shard_map/ppermute | solution.py:58
  4.0 0.0 collective-permute-start.1
  4.0 3.0 %collective-permute-done = bf16[8,7680]{1,0:T(8,128)(2,1)S(1)} collective-permute-done((bf16[8,7680]{1,0:T(8,128)(2,1)S(1)}, bf16[8,7680]{1,0:T(8,128)(2,1)S(1)}, u32[]{:S(2)}, u32[]{:S(2)}) %collective-permute-start) | collective-permute-done | bytes 122912 | tf_op jit(solution)/shard_map/ppermute | solution.py:58
  7.0 1.2 %collective-permute-start.2 = (bf16[8,7680]{1,0:T(8,128)(2,1)S(1)}, bf16[8,7680]{1,0:T(8,128)(2,1)S(1)}, u32[]{:S(2)}, u32[]{:S(2)}) collective-permute-start(bf16[8,7680]{1,0:T(8,128)(2,1)S(1)} %collective-permute-done), channel_id=1, source_target_pairs={{0,4},{2,0},{4,8},{6,2},{8,12},{10,6},{12,14},{14,10},{1,5},{3,1},... | collective-permute-start | bytes 368648 | tf_op jit(solution)/shard_map/ppermute | solution.py:58
  8.2 0.0 collective-permute-done.1
  8.2 0.2 collective-permute-start.3
  8.5 2.3 %collective-permute-done.2 = bf16[8,7680]{1,0:T(8,128)(2,1)S(1)} collective-permute-done((bf16[8,7680]{1,0:T(8,128)(2,1)S(1)}, bf16[8,7680]{1,0:T(8,128)(2,1)S(1)}, u32[]{:S(2)}, u32[]{:S(2)}) %collective-permute-start.2) | collective-permute-done | bytes 122912 | tf_op jit(solution)/shard_map/ppermute | solution.py:58
  10.7 1.2 %collective-permute-start.4 = (bf16[8,7680]{1,0:T(8,128)(2,1)S(1)}, bf16[8,7680]{1,0:T(8,128)(2,1)S(1)}, u32[]{:S(2)}, u32[]{:S(2)}) collective-permute-start(bf16[8,7680]{1,0:T(8,128)(2,1)S(1)} %collective-permute-done.2), channel_id=1, source_target_pairs={{0,4},{2,0},{4,8},{6,2},{8,12},{10,6},{12,14},{14,10},{1,5},{3,1},... | collective-permute-start | bytes 368648 | tf_op jit(solution)/shard_map/ppermute | solution.py:58
  12.0 0.3 collective-permute-done.3
  12.3 0.0 collective-permute-start.5
  12.3 2.3 %collective-permute-done.4 = bf16[8,7680]{1,0:T(8,128)(2,1)S(1)} collective-permute-done((bf16[8,7680]{1,0:T(8,128)(2,1)S(1)}, bf16[8,7680]{1,0:T(8,128)(2,1)S(1)}, u32[]{:S(2)}, u32[]{:S(2)}) %collective-permute-start.4) | collective-permute-done | bytes 122912 | tf_op jit(solution)/shard_map/ppermute | solution.py:58
  14.5 1.3 %collective-permute-start.6 = (bf16[8,7680]{1,0:T(8,128)(2,1)S(1)}, bf16[8,7680]{1,0:T(8,128)(2,1)S(1)}, u32[]{:S(2)}, u32[]{:S(2)}) collective-permute-start(bf16[8,7680]{1,0:T(8,128)(2,1)S(1)} %collective-permute-done.4), channel_id=1, source_target_pairs={{0,4},{2,0},{4,8},{6,2},{8,12},{10,6},{12,14},{14,10},{1,5},{3,1},... | collective-permute-start | bytes 368648 | tf_op jit(solution)/shard_map/ppermute | solution.py:58
  15.8 0.4 collective-permute-done.5
  16.3 2.6 %collective-permute-done.6 = bf16[8,7680]{1,0:T(8,128)(2,1)S(1)} collective-permute-done((bf16[8,7680]{1,0:T(8,128)(2,1)S(1)}, bf16[8,7680]{1,0:T(8,128)(2,1)S(1)}, u32[]{:S(2)}, u32[]{:S(2)}) %collective-permute-start.6) | collective-permute-done | bytes 122912 | tf_op jit(solution)/shard_map/ppermute | solution.py:58
  18.9 0.1 assemble.1
  19.1 4.5 %collective-permute-start.7 = (bf16[80,1536]{1,0:T(8,128)(2,1)S(1)}, bf16[80,1536]{1,0:T(8,128)(2,1)S(1)}, u32[]{:S(2)}, u32[]{:S(2)}) collective-permute-start(bf16[80,1536]{1,0:T(8,128)(2,1)S(1)} %get-tuple-element.7.own_ref), channel_id=1, source_target_pairs={{0,1},{1,0},{2,3},{3,2},{4,5},{5,4},{6,7},{7,6},{8,9},{9,8},{10,11... | collective-permute-start | bytes 737288 | tf_op jit(solution)/shard_map/ppermute | solution.py:191
  23.6 1.1 %collective-permute-done.7.peer_ref = bf16[80,1536]{1,0:T(8,128)(2,1)S(1)} collective-permute-done((bf16[80,1536]{1,0:T(8,128)(2,1)S(1)}, bf16[80,1536]{1,0:T(8,128)(2,1)S(1)}, u32[]{:S(2)}, u32[]{:S(2)}) %collective-permute-start.7) | collective-permute-done | bytes 245792 | tf_op jit(solution)/shard_map/ppermute | solution.py:191
  24.7 0.0 copy-start
  24.7 11.7 %copy-done = f32[1536,6144]{1,0:T(8,128)S(1)} copy-done((f32[1536,6144]{1,0:T(8,128)S(1)}, f32[1536,6144]{1,0:T(8,128)}, u32[]{:S(2)}) %copy-start) | copy-done | bytes 37748760
  36.5 12.8 %update.1 = f32[1536,6144]{1,0:T(8,128)} custom-call(f32[1536,6144]{1,0:T(8,128)S(1)} %copy-done, bf16[80,1536]{1,0:T(8,128)(2,1)S(1)} %get-tuple-element.7.own_ref, bf16[80,1536]{1,0:T(8,128)(2,1)S(1)} %collective-permute-done.7.peer_ref, bf16[80,6144]{1,0:T(8,128)(2,1)S(1)} %get-tuple-element.8.right_ref), custom_call_target="tpu_custom_call" | custom-call | tf_op jit(solution)/shard_map/update/pallas_call | solution.py:166
Async XLA Ops:
  0.0 0.9 %copy-start.1 = (bf16[5,6144]{1,0:T(8,128)(2,1)S(1)}, bf16[5,6144]{1,0:T(8,128)(2,1)}, u32[]{:S(2)}) copy-start(bf16[5,6144]{1,0:T(8,128)(2,1)} %first_ref.1) | copy-start | bytes 184324
  0.9 0.9 %copy-start.2 = (bf16[5,6144]{1,0:T(8,128)(2,1)S(1)}, bf16[5,6144]{1,0:T(8,128)(2,1)}, u32[]{:S(2)}) copy-start(bf16[5,6144]{1,0:T(8,128)(2,1)} %second_ref.1) | copy-start | bytes 184324
  1.9 5.1 %collective-permute-start = (bf16[8,7680]{1,0:T(8,128)(2,1)S(1)}, bf16[8,7680]{1,0:T(8,128)(2,1)S(1)}, u32[]{:S(2)}, u32[]{:S(2)}) collective-permute-start(bf16[8,7680]{1,0:T(8,128)(2,1)S(1)} %pack.1), channel_id=1, source_target_pairs={{0,4},{2,0},{4,8},{6,2},{8,12},{10,6},{12,14},{14,10},{1,5},{3,1},... | collective-permute-start | bytes 368648 | tf_op jit(solution)/shard_map/ppermute | solution.py:58
  4.0 4.2 %collective-permute-start.1 = (bf16[8,7680]{1,0:T(8,128)(2,1)S(1)}, bf16[8,7680]{1,0:T(8,128)(2,1)S(1)}, u32[]{:S(2)}, u32[]{:S(2)}) collective-permute-start(bf16[8,7680]{1,0:T(8,128)(2,1)S(1)} %pack.1), channel_id=1, source_target_pairs={{0,2},{2,6},{4,0},{6,10},{8,4},{10,14},{12,8},{14,12},{1,3},{3,7},... | collective-permute-start | bytes 368648 | tf_op jit(solution)/shard_map/ppermute | solution.py:58
  7.0 3.7 %collective-permute-start.2 = (bf16[8,7680]{1,0:T(8,128)(2,1)S(1)}, bf16[8,7680]{1,0:T(8,128)(2,1)S(1)}, u32[]{:S(2)}, u32[]{:S(2)}) collective-permute-start(bf16[8,7680]{1,0:T(8,128)(2,1)S(1)} %collective-permute-done), channel_id=1, source_target_pairs={{0,4},{2,0},{4,8},{6,2},{8,12},{10,6},{12,14},{14,10},{1,5},{3,1},... | collective-permute-start | bytes 368648 | tf_op jit(solution)/shard_map/ppermute | solution.py:58
  8.2 4.0 %collective-permute-start.3 = (bf16[8,7680]{1,0:T(8,128)(2,1)S(1)}, bf16[8,7680]{1,0:T(8,128)(2,1)S(1)}, u32[]{:S(2)}, u32[]{:S(2)}) collective-permute-start(bf16[8,7680]{1,0:T(8,128)(2,1)S(1)} %collective-permute-done.1), channel_id=1, source_target_pairs={{0,2},{2,6},{4,0},{6,10},{8,4},{10,14},{12,8},{14,12},{1,3},{3,7},... | collective-permute-start | bytes 368648 | tf_op jit(solution)/shard_map/ppermute | solution.py:58
  10.7 3.8 %collective-permute-start.4 = (bf16[8,7680]{1,0:T(8,128)(2,1)S(1)}, bf16[8,7680]{1,0:T(8,128)(2,1)S(1)}, u32[]{:S(2)}, u32[]{:S(2)}) collective-permute-start(bf16[8,7680]{1,0:T(8,128)(2,1)S(1)} %collective-permute-done.2), channel_id=1, source_target_pairs={{0,4},{2,0},{4,8},{6,2},{8,12},{10,6},{12,14},{14,10},{1,5},{3,1},... | collective-permute-start | bytes 368648 | tf_op jit(solution)/shard_map/ppermute | solution.py:58
  12.3 4.0 %collective-permute-start.5 = (bf16[8,7680]{1,0:T(8,128)(2,1)S(1)}, bf16[8,7680]{1,0:T(8,128)(2,1)S(1)}, u32[]{:S(2)}, u32[]{:S(2)}) collective-permute-start(bf16[8,7680]{1,0:T(8,128)(2,1)S(1)} %collective-permute-done.3), channel_id=1, source_target_pairs={{0,2},{2,6},{4,0},{6,10},{8,4},{10,14},{12,8},{14,12},{1,3},{3,7},... | collective-permute-start | bytes 368648 | tf_op jit(solution)/shard_map/ppermute | solution.py:58
  14.5 4.4 %collective-permute-start.6 = (bf16[8,7680]{1,0:T(8,128)(2,1)S(1)}, bf16[8,7680]{1,0:T(8,128)(2,1)S(1)}, u32[]{:S(2)}, u32[]{:S(2)}) collective-permute-start(bf16[8,7680]{1,0:T(8,128)(2,1)S(1)} %collective-permute-done.4), channel_id=1, source_target_pairs={{0,4},{2,0},{4,8},{6,2},{8,12},{10,6},{12,14},{14,10},{1,5},{3,1},... | collective-permute-start | bytes 368648 | tf_op jit(solution)/shard_map/ppermute | solution.py:58
  19.1 5.7 %collective-permute-start.7 = (bf16[80,1536]{1,0:T(8,128)(2,1)S(1)}, bf16[80,1536]{1,0:T(8,128)(2,1)S(1)}, u32[]{:S(2)}, u32[]{:S(2)}) collective-permute-start(bf16[80,1536]{1,0:T(8,128)(2,1)S(1)} %get-tuple-element.7.own_ref), channel_id=1, source_target_pairs={{0,1},{1,0},{2,3},{3,2},{4,5},{5,4},{6,7},{7,6},{8,9},{9,8},{10,11... | collective-permute-start | bytes 737288 | tf_op jit(solution)/shard_map/ppermute | solution.py:191
  24.7 11.7 %copy-start = (f32[1536,6144]{1,0:T(8,128)S(1)}, f32[1536,6144]{1,0:T(8,128)}, u32[]{:S(2)}) copy-start(f32[1536,6144]{1,0:T(8,128)} %schur_ref.1) | copy-start | bytes 113246208

commit v2 on v1

v2 whole, which is shorter than its diff:
```python
import functools

import jax
import jax.numpy as jnp
from jax import lax
from jax.experimental import pallas as pl
from jax.experimental.pallas import tpu as pltpu
from jax.sharding import PartitionSpec as P

MIB = 1 << 20
WHOLE = pl.BlockSpec(memory_space=pltpu.VMEM)
ANYWHERE = pl.BlockSpec(memory_space=pl.ANY)
IN_HBM = pl.BlockSpec(memory_space=pltpu.HBM)
SHARES = ([5, 5, 5, 5], 2, 2)
COLS = 1024


def in_vmem(array):
    return pltpu.with_memory_space_constraint(array, pltpu.VMEM)


def in_hbm(array):
    return pltpu.with_memory_space_constraint(array, pltpu.HBM)


class Packing:
    def __init__(self, rows, width):
        self.rows, self.width = rows, width
        self.full = rows // 8 * 8
        self.rest = rows - self.full
        self.fold = 8 // self.rest if self.rest else 1
        assert self.rest == 0 or (8 % self.rest == 0 and self.full == 8)
        assert width % (128 * self.fold) == 0
        self.chunk = width // self.fold
        self.packed = (self.full, width + (self.chunk if self.rest else 0))


def pack_kernel(packing, first_hbm, second_hbm, out_ref, first_ref, second_ref, sems):
    copies = [
        pltpu.make_async_copy(first_hbm, first_ref, sems.at[0]),
        pltpu.make_async_copy(second_hbm, second_ref, sems.at[1]),
    ]
    for copy in copies:
        copy.start()
    for copy in copies:
        copy.wait()
    both = jnp.concatenate([first_ref[...], second_ref[...]], axis=0)
    out_ref[:, : packing.width] = both[: packing.full]
    for i in range(packing.fold if packing.rest else 0):
        lanes = slice(i * packing.chunk, (i + 1) * packing.chunk)
        out_ref[i * packing.rest : (i + 1) * packing.rest, packing.width :] = both[packing.full :, lanes]


def pack(packing, first, second):
    return pl.pallas_call(
        functools.partial(pack_kernel, packing),
        in_specs=[IN_HBM] * 2,
        out_specs=WHOLE,
        out_shape=pltpu.VMEM(packing.packed, first.dtype),
        scratch_shapes=[
            pltpu.VMEM(first.shape, first.dtype),
            pltpu.VMEM(second.shape, second.dtype),
            pltpu.SemaphoreType.DMA((2,)),
        ],
        compiler_params=pltpu.CompilerParams(vmem_limit_bytes=8 * MIB),
        name="pack",
    )(in_hbm(first), in_hbm(second))


def fetch_kernel(low, schur_ref, token_ref, out_ref, sem):
    copy = pltpu.make_async_copy(schur_ref.at[pl.ds(low, out_ref.shape[0]), :], out_ref, sem)
    copy.start()
    copy.wait()


def fetch(schur, low, rows, token):
    width = schur.shape[1]
    return pl.pallas_call(
        functools.partial(fetch_kernel, low),
        in_specs=[IN_HBM, ANYWHERE],
        out_specs=WHOLE,
        out_shape=pltpu.VMEM((rows, width), schur.dtype),
        scratch_shapes=[pltpu.SemaphoreType.DMA],
        cost_estimate=pl.CostEstimate(flops=0, transcendentals=0, bytes_accessed=8 * rows * width),
        compiler_params=pltpu.CompilerParams(vmem_limit_bytes=MIB),
        name="fetch",
    )(in_hbm(schur), token)


def shares_of(rows, hops):
    by_hop, by_swap, late = SHARES
    unit = rows // (sum(by_hop) + by_swap + late)
    if hops != len(by_hop) or unit % 16 or unit * (sum(by_hop) + by_swap + late) != rows:
        return [], rows
    return [s * unit for s in by_hop], by_swap * unit


def gather_rows(block, axis, schur, sizes):
    count = lax.axis_size(axis)
    if not sizes:
        return [lax.all_gather(block, axis, axis=0)], []
    ring = [2 * i for i in range(count // 2)] + [2 * i + 1 for i in reversed(range(count // 2))]
    place = {index: position for position, index in enumerate(ring)}

    def step(array, by):
        return lax.ppermute(array, axis, [(i, ring[(place[i] + by) % count]) for i in range(count)])

    blocks, ahead, behind, fetched = [block], block, block, []
    for hop in range(count // 2):
        part = fetch(schur, sum(sizes[:hop]), sizes[hop], ahead)
        ahead = step(ahead, 1)
        if hop < count // 2 - 1:
            behind = step(behind, -1)
        ahead, part = lax.optimization_barrier((ahead, part))
        if hop < count // 2 - 1:
            behind, part = lax.optimization_barrier((behind, part))
        blocks.append(ahead)
        if hop < count // 2 - 1:
            blocks.append(behind)
        fetched.append(part)
    return [b[None] for b in blocks], fetched


def assemble_kernel(packing, tile, per_column, *refs):
    *piece_refs, right_ref, left_ref = refs
    count = sum(ref.shape[0] for ref in piece_refs)
    at = 0
    for ref in piece_refs:
        for p in range(ref.shape[0]):
            right_ref[at * packing.full : (at + 1) * packing.full, :] = ref[p, :, : packing.width]
            for i in range(packing.fold if packing.rest else 0):
                lanes = slice(i * packing.chunk, (i + 1) * packing.chunk)
                low = count * packing.full + at * packing.rest
                right_ref[low : low + packing.rest, lanes] = ref[
                    p, i * packing.rest : (i + 1) * packing.rest, packing.width :
                ]
            at += 1
    start = pl.multiple_of(lax.axis_index("row") % per_column * tile, 128)
    left_ref[...] = right_ref[:, pl.ds(start, tile)]


def assemble(packing, pieces, tile, per_column):
    depth = packing.rows * sum(p.shape[0] for p in pieces)
    dtype = pieces[0].dtype
    return pl.pallas_call(
        functools.partial(assemble_kernel, packing, tile, per_column),
        in_specs=[WHOLE] * len(pieces),
        out_specs=(WHOLE, WHOLE),
        out_shape=(pltpu.VMEM((depth, packing.width), dtype), pltpu.VMEM((depth, tile), dtype)),
        compiler_params=pltpu.CompilerParams(vmem_limit_bytes=8 * MIB),
        name="assemble",
    )(*[in_vmem(p) for p in pieces])


def assemble_plain(packing, pieces, tile, per_column):
    stack = jnp.concatenate(pieces, axis=0)
    count = stack.shape[0]
    top = stack[:, :, : packing.width].reshape(count * packing.full, packing.width)
    rest = stack[:, :, packing.width :].reshape(count, packing.fold, packing.rest, packing.chunk)
    rest = jnp.transpose(rest, (0, 2, 1, 3)).reshape(count * packing.rest, packing.width)
    right = jnp.concatenate([top, rest], axis=0)
    start = lax.axis_index("row") % per_column * tile
    return right, lax.dynamic_slice(right, (0, start), (right.shape[0], tile))


def update_kernel(columns, per_column, schur_hbm, own_ref, peer_ref, right_ref, *refs):
    count = (len(refs) - 5) // 2
    parts, out_ref, held = refs[:count], refs[count], list(refs[count + 1 : 2 * count + 1])
    left, late, sems, late_sem = refs[2 * count + 1 :]
    width = out_ref.shape[1]
    late_rows = out_ref.shape[0] - sum(part.shape[0] for part in parts)
    owner = lax.axis_index("col") == lax.axis_index("row") // per_column
    if late_rows:
        fill = pltpu.make_async_copy(schur_hbm.at[pl.ds(out_ref.shape[0] - late_rows, late_rows), :], late, late_sem)
        fill.start()
        parts, held = [*parts, late], [*held, late]
    steps = width // columns
    lows = [sum(part.shape[0] for part in parts[:i]) for i in range(len(parts))]

    def copy(number, t):
        rows = parts[number].shape[0]
        lanes = pl.ds(pl.multiple_of(t * columns, columns), columns)
        return pltpu.make_async_copy(
            held[number].at[:, lanes], out_ref.at[pl.ds(lows[number], rows), lanes], sems.at[number, t]
        )

    for number, part in enumerate(parts):
        low, rows = lows[number], part.shape[0]

        @pl.when(owner)
        def _():
            left[:rows, :] = own_ref[:, low : low + rows].T

        @pl.when(jnp.logical_not(owner))
        def _():
            left[:rows, :] = peer_ref[:, low : low + rows].T

        if late_rows and number == len(parts) - 1:
            fill.wait()

        def step(t, _):
            lanes = pl.ds(pl.multiple_of(t * columns, columns), columns)
            update = jnp.dot(left[:rows, :], right_ref[:, lanes], preferred_element_type=jnp.float32)
            held[number][:, lanes] = part[:, lanes] - update
            copy(number, t).start()
            return 0

        lax.fori_loop(0, steps, step, 0)
    for number in range(len(parts)):
        for t in range(steps):
            copy(number, t).wait()


def update(schur, parts, own, peer, right, per_column):
    depth, width = right.shape
    tile = schur.shape[0]
    late_rows = tile - sum(part.shape[0] for part in parts)
    columns = next(c for c in (COLS, 256, 128) if width % c == 0)
    most = max([part.shape[0] for part in parts] + [late_rows])
    scratch = 2 * most * max(depth, 128) + 4 * late_rows * width
    result, *_ = pl.pallas_call(
        functools.partial(update_kernel, columns, per_column),
        in_specs=[IN_HBM] + [WHOLE] * (3 + len(parts)),
        out_specs=[ANYWHERE] + [WHOLE] * len(parts),
        out_shape=[jax.ShapeDtypeStruct(schur.shape, schur.dtype)] + [pltpu.VMEM(p.shape, p.dtype) for p in parts],
        input_output_aliases={4 + i: 1 + i for i in range(len(parts))},
        scratch_shapes=[
            pltpu.VMEM((most, depth), right.dtype),
            pltpu.VMEM((late_rows or 8, width), jnp.float32),
            pltpu.SemaphoreType.DMA((len(parts) + 1, width // columns)),
            pltpu.SemaphoreType.DMA,
        ],
        compiler_params=pltpu.CompilerParams(vmem_limit_bytes=scratch + 4 * MIB),
        name="update",
    )(in_hbm(schur), *[in_vmem(a) for a in (own, peer, right, *parts)])
    return result


def per_device(schur_block, w_first, w_second):
    row_count = lax.axis_size("row")
    col_count = lax.axis_size("col")
    tile, width = schur_block.shape
    per_column = row_count // col_count
    packing = Packing(w_first.shape[0] + w_second.shape[0], width)
    sizes, beside_swap = shares_of(tile, row_count // 2)
    pieces, parts = gather_rows(pack(packing, w_first, w_second), "row", schur_block, sizes)
    build = assemble if tile % 128 == 0 else assemble_plain
    right, own = build(packing, pieces, tile, per_column)
    if beside_swap:
        parts = [*parts, fetch(schur_block, sum(sizes), beside_swap, own)]
    peer = lax.ppermute(own, "col", [(c, (c + 1) % col_count) for c in range(col_count)])
    return update(schur_block, parts, own, peer, right, per_column)


def solution(mesh):
    assert mesh.shape["col"] == 2
    placed = P(("sup", "row"), "col")
    return jax.shard_map(per_device, mesh=mesh, in_specs=(placed,) * 3, out_specs=placed, check_vma=False)
```

time: 49.8 us -> 38.8 us (0.78)
  Pallas kernels: 13 us -> 28.9 us
  local copies, waits for them, and re-layouts: 13.5 us -> 0 us
  waiting for transfers between devices: 12 us -> 0.02 us
  starting transfers between devices: 10.7 us -> 9.42 us
    pallas_call x2 -> x7, Pallas kernels: 12.8 us -> 28.8 us  [the longest x5 14.9 us: fetch(): pl.pallas_call(functools.partial(fetch_kernel, low), in_specs=[IN_HBM, AN...]
    unnamed x6 -> x0, local copies, waits for them, and re-layouts: 13.5 us -> none
    ppermute x7, waiting for transfers between devices: 10.9 us -> 0.02 us  [step(): lax.ppermute(array, axis, [(i, ring[(place[i] + by) % count]) for i in ra...]
    ppermute x1, starting transfers between devices: 4.54 us -> 2.7 us  [per_device(): lax.ppermute(own, 'col', [(c, (c + 1) % col_count) for c in range(col_cou...]
    ppermute x1, waiting for transfers between devices: 1.14 us -> 0.01 us  [per_device(): lax.ppermute(own, 'col', [(c, (c + 1) % col_count) for c in range(col_cou...]
    ppermute x7, starting transfers between devices: 6.17 us -> 6.72 us  [step(): lax.ppermute(array, axis, [(i, ring[(place[i] + by) % count]) for i in ra...]
  transfers between devices with their start and end apart: 8 -> 8, of which waited for: 7 -> 0; matrix products, arithmetic and copies ran while one was open for 0% -> 0% of each run, Pallas kernels for 0% -> 39%
where the time goes in v2:
time: 38.8 us; the launch traced here: 38.5 us
  Pallas kernels  28.9 us (74%)
  starting transfers between devices  9.42 us (24%)
    pallas_call x5, Pallas kernels, fetch(): pl.pallas_call(functools.partial(fetch_kernel, low), in_specs=[IN_HBM, AN...  14.9 us
    pallas_call x1, Pallas kernels, update(): pl.pallas_call(functools.partial(update_kernel, columns, per_column), in_...  12.9 us
    ppermute x7, starting transfers between devices, step(): lax.ppermute(array, axis, [(i, ring[(place[i] + by) % count]) for i in ra...  6.72 us
    ppermute x1, starting transfers between devices, per_device(): lax.ppermute(own, 'col', [(c, (c + 1) % col_count) for c in range(col_cou...  2.7 us
    pallas_call x1, Pallas kernels, pack(): pl.pallas_call(functools.partial(pack_kernel, packing), in_specs=[IN_HBM]...  1.02 us
  transfers between devices with their start and end apart: 8, of which 0 were waited for; matrix products, arithmetic and copies ran while one was open for 0% of the time, Pallas kernels for 39%

profile of v2, /device:TPU:1, one launch (start us, length us, event | category | flops | bytes accessed | tf_op | source)
XLA Modules:
  0.0 38.5 jit_solution(2112819336095569115)
XLA Ops:
  0.0 1.0 %pack.1.token_ref = bf16[8,7680]{1,0:T(8,128)(2,1)S(1)} custom-call(bf16[5,6144]{1,0:T(8,128)(2,1)} %first_hbm.1, bf16[5,6144]{1,0:T(8,128)(2,1)} %second_hbm.1), custom_call_target="tpu_custom_call" | custom-call | tf_op jit(solution)/shard_map/pack/pallas_call | solution.py:55
  1.0 2.2 %collective-permute-start = (bf16[8,7680]{1,0:T(8,128)(2,1)S(1)}, bf16[8,7680]{1,0:T(8,128)(2,1)S(1)}, u32[]{:S(2)}, u32[]{:S(2)}) collective-permute-start(bf16[8,7680]{1,0:T(8,128)(2,1)S(1)} %pack.1.token_ref), channel_id=1, source_target_pairs={{0,4},{2,0},{4,8},{6,2},{8,12},{10,6},{12,14},{14,10},{1,5},{3,1},... | collective-permute-start | bytes 368648 | tf_op jit(solution)/shard_map/ppermute | solution.py:106
  3.2 0.0 collective-permute-start.1
  3.2 3.2 %fetch.5.refs_0_ = f32[320,6144]{1,0:T(8,128)S(1)} custom-call(f32[1536,6144]{1,0:T(8,128)} %schur_hbm.1, bf16[8,7680]{1,0:T(8,128)(2,1)S(1)} %pack.1.token_ref), custom_call_target="tpu_custom_call" | custom-call | bytes 15728640 | tf_op jit(solution)/shard_map/fetch/pallas_call | solution.py:78
  6.5 0.0 collective-permute-done.token_ref
  6.5 1.5 %collective-permute-start.2 = (bf16[8,7680]{1,0:T(8,128)(2,1)S(1)}, bf16[8,7680]{1,0:T(8,128)(2,1)S(1)}, u32[]{:S(2)}, u32[]{:S(2)}) collective-permute-start(bf16[8,7680]{1,0:T(8,128)(2,1)S(1)} %collective-permute-done.token_ref), channel_id=1, source_target_pairs={{0,4},{2,0},{4,8},{6,2},{8,12},{10,6},{12,14},{14,10},{1,5},{3,1},... | collective-permute-start | bytes 368648 | tf_op jit(solution)/shard_map/ppermute | solution.py:106
  8.0 0.0 collective-permute-done.1
  8.0 0.0 collective-permute-start.3
  8.0 3.2 %fetch.6.refs_1_ = f32[320,6144]{1,0:T(8,128)S(1)} custom-call(f32[1536,6144]{1,0:T(8,128)} %schur_hbm.1, bf16[8,7680]{1,0:T(8,128)(2,1)S(1)} %collective-permute-done.token_ref), custom_call_target="tpu_custom_call" | custom-call | bytes 15728640 | tf_op jit(solution)/shard_map/fetch/pallas_call | solution.py:78
  11.2 0.0 collective-permute-done.2.token_ref
  11.2 1.5 %collective-permute-start.4 = (bf16[8,7680]{1,0:T(8,128)(2,1)S(1)}, bf16[8,7680]{1,0:T(8,128)(2,1)S(1)}, u32[]{:S(2)}, u32[]{:S(2)}) collective-permute-start(bf16[8,7680]{1,0:T(8,128)(2,1)S(1)} %collective-permute-done.2.token_ref), channel_id=1, source_target_pairs={{0,4},{2,0},{4,8},{6,2},{8,12},{10,6},{12,14},{14,10},{1,5},{3,1},... | collective-permute-start | bytes 368648 | tf_op jit(solution)/shard_map/ppermute | solution.py:106
  12.8 3.2 %fetch.7.refs_2_ = f32[320,6144]{1,0:T(8,128)S(1)} custom-call(f32[1536,6144]{1,0:T(8,128)} %schur_hbm.1, bf16[8,7680]{1,0:T(8,128)(2,1)S(1)} %collective-permute-done.2.token_ref), custom_call_target="tpu_custom_call" | custom-call | bytes 15728640 | tf_op jit(solution)/shard_map/fetch/pallas_call | solution.py:78
  16.0 0.0 collective-permute-done.3
  16.0 0.1 collective-permute-start.5
  16.1 0.0 collective-permute-done.4.token_ref
  16.1 1.4 %collective-permute-start.6 = (bf16[8,7680]{1,0:T(8,128)(2,1)S(1)}, bf16[8,7680]{1,0:T(8,128)(2,1)S(1)}, u32[]{:S(2)}, u32[]{:S(2)}) collective-permute-start(bf16[8,7680]{1,0:T(8,128)(2,1)S(1)} %collective-permute-done.4.token_ref), channel_id=1, source_target_pairs={{0,4},{2,0},{4,8},{6,2},{8,12},{10,6},{12,14},{14,10},{1,5},{3,1},... | collective-permute-start | bytes 368648 | tf_op jit(solution)/shard_map/ppermute | solution.py:106
  17.5 3.2 %fetch.8.refs_3_ = f32[320,6144]{1,0:T(8,128)S(1)} custom-call(f32[1536,6144]{1,0:T(8,128)} %schur_hbm.1, bf16[8,7680]{1,0:T(8,128)(2,1)S(1)} %collective-permute-done.4.token_ref), custom_call_target="tpu_custom_call" | custom-call | bytes 15728640 | tf_op jit(solution)/shard_map/fetch/pallas_call | solution.py:78
  20.8 0.0 collective-permute-done.5
  20.8 0.0 collective-permute-done.6
  20.8 0.1 assemble.1
  21.0 2.7 %collective-permute-start.7 = (bf16[80,1536]{1,0:T(8,128)(2,1)S(1)}, bf16[80,1536]{1,0:T(8,128)(2,1)S(1)}, u32[]{:S(2)}, u32[]{:S(2)}) collective-permute-start(bf16[80,1536]{1,0:T(8,128)(2,1)S(1)} %get-tuple-element.32.token_ref.own_ref), channel_id=1, source_target_pairs={{0,1},{1,0},{2,3},{3,2},{4,5},{5,4},{6,7},{7,6},{8,9},{9,8},{10,11... | collective-permute-start | bytes 737288 | tf_op jit(solution)/shard_map/ppermute | solution.py:251
  23.7 1.9 %fetch.9.refs_4_ = f32[128,6144]{1,0:T(8,128)S(1)} custom-call(f32[1536,6144]{1,0:T(8,128)} %schur_hbm.1, bf16[80,1536]{1,0:T(8,128)(2,1)S(1)} %get-tuple-element.32.token_ref.own_ref), custom_call_target="tpu_custom_call" | custom-call | bytes 6291456 | tf_op jit(solution)/shard_map/fetch/pallas_call | solution.py:78
  25.6 0.0 collective-permute-done.7.peer_ref
  25.6 12.9 %update.1 = (f32[1536,6144]{1,0:T(8,128)}, f32[320,6144]{1,0:T(8,128)S(1)}, f32[320,6144]{1,0:T(8,128)S(1)}, f32[320,6144]{1,0:T(8,128)S(1)}, f32[320,6144]{1,0:T(8,128)S(1)}, /*index=5*/f32[128,6144]{1,0:T(8,128)S(1)}) custom-call(f32[1536,6144]{1,0:T(8,128)} %schur_hbm.1, ...), custom_call_target="tpu_custom_call", output_to_operand_aliasing={{1}: (4, {}), {2}: (5, {}), {3}: (6, {}), {4}: (7, {}), {5}... | custom-call | tf_op jit(solution)/shard_map/update/pallas_call | solution.py:221
Async XLA Ops:
  1.0 5.4 %collective-permute-start = (bf16[8,7680]{1,0:T(8,128)(2,1)S(1)}, bf16[8,7680]{1,0:T(8,128)(2,1)S(1)}, u32[]{:S(2)}, u32[]{:S(2)}) collective-permute-start(bf16[8,7680]{1,0:T(8,128)(2,1)S(1)} %pack.1.token_ref), channel_id=1, source_target_pairs={{0,4},{2,0},{4,8},{6,2},{8,12},{10,6},{12,14},{14,10},{1,5},{3,1},... | collective-permute-start | bytes 368648 | tf_op jit(solution)/shard_map/ppermute | solution.py:106
  3.2 4.8 %collective-permute-start.1 = (bf16[8,7680]{1,0:T(8,128)(2,1)S(1)}, bf16[8,7680]{1,0:T(8,128)(2,1)S(1)}, u32[]{:S(2)}, u32[]{:S(2)}) collective-permute-start(bf16[8,7680]{1,0:T(8,128)(2,1)S(1)} %pack.1.token_ref), channel_id=1, source_target_pairs={{0,2},{2,6},{4,0},{6,10},{8,4},{10,14},{12,8},{14,12},{1,3},{3,7},... | collective-permute-start | bytes 368648 | tf_op jit(solution)/shard_map/ppermute | solution.py:106
  6.5 4.8 %collective-permute-start.2 = (bf16[8,7680]{1,0:T(8,128)(2,1)S(1)}, bf16[8,7680]{1,0:T(8,128)(2,1)S(1)}, u32[]{:S(2)}, u32[]{:S(2)}) collective-permute-start(bf16[8,7680]{1,0:T(8,128)(2,1)S(1)} %collective-permute-done.token_ref), channel_id=1, source_target_pairs={{0,4},{2,0},{4,8},{6,2},{8,12},{10,6},{12,14},{14,10},{1,5},{3,1},... | collective-permute-start | bytes 368648 | tf_op jit(solution)/shard_map/ppermute | solution.py:106
  8.0 8.0 %collective-permute-start.3 = (bf16[8,7680]{1,0:T(8,128)(2,1)S(1)}, bf16[8,7680]{1,0:T(8,128)(2,1)S(1)}, u32[]{:S(2)}, u32[]{:S(2)}) collective-permute-start(bf16[8,7680]{1,0:T(8,128)(2,1)S(1)} %collective-permute-done.1), channel_id=1, source_target_pairs={{0,2},{2,6},{4,0},{6,10},{8,4},{10,14},{12,8},{14,12},{1,3},{3,7},... | collective-permute-start | bytes 368648 | tf_op jit(solution)/shard_map/ppermute | solution.py:106
  11.2 4.8 %collective-permute-start.4 = (bf16[8,7680]{1,0:T(8,128)(2,1)S(1)}, bf16[8,7680]{1,0:T(8,128)(2,1)S(1)}, u32[]{:S(2)}, u32[]{:S(2)}) collective-permute-start(bf16[8,7680]{1,0:T(8,128)(2,1)S(1)} %collective-permute-done.2.token_ref), channel_id=1, source_target_pairs={{0,4},{2,0},{4,8},{6,2},{8,12},{10,6},{12,14},{14,10},{1,5},{3,1},... | collective-permute-start | bytes 368648 | tf_op jit(solution)/shard_map/ppermute | solution.py:106
  16.0 4.8 %collective-permute-start.5 = (bf16[8,7680]{1,0:T(8,128)(2,1)S(1)}, bf16[8,7680]{1,0:T(8,128)(2,1)S(1)}, u32[]{:S(2)}, u32[]{:S(2)}) collective-permute-start(bf16[8,7680]{1,0:T(8,128)(2,1)S(1)} %collective-permute-done.3), channel_id=1, source_target_pairs={{0,2},{2,6},{4,0},{6,10},{8,4},{10,14},{12,8},{14,12},{1,3},{3,7},... | collective-permute-start | bytes 368648 | tf_op jit(solution)/shard_map/ppermute | solution.py:106
  16.1 4.7 %collective-permute-start.6 = (bf16[8,7680]{1,0:T(8,128)(2,1)S(1)}, bf16[8,7680]{1,0:T(8,128)(2,1)S(1)}, u32[]{:S(2)}, u32[]{:S(2)}) collective-permute-start(bf16[8,7680]{1,0:T(8,128)(2,1)S(1)} %collective-permute-done.4.token_ref), channel_id=1, source_target_pairs={{0,4},{2,0},{4,8},{6,2},{8,12},{10,6},{12,14},{14,10},{1,5},{3,1},... | collective-permute-start | bytes 368648 | tf_op jit(solution)/shard_map/ppermute | solution.py:106
  21.0 4.6 %collective-permute-start.7 = (bf16[80,1536]{1,0:T(8,128)(2,1)S(1)}, bf16[80,1536]{1,0:T(8,128)(2,1)S(1)}, u32[]{:S(2)}, u32[]{:S(2)}) collective-permute-start(bf16[80,1536]{1,0:T(8,128)(2,1)S(1)} %get-tuple-element.32.token_ref.own_ref), channel_id=1, source_target_pairs={{0,1},{1,0},{2,3},{3,2},{4,5},{5,4},{6,7},{7,6},{8,9},{9,8},{10,11... | collective-permute-start | bytes 737288 | tf_op jit(solution)/shard_map/ppermute | solution.py:251

commit v3 on v2

--- a/solution.py
+++ b/solution.py
@@ -11,8 +11,9 @@
 WHOLE = pl.BlockSpec(memory_space=pltpu.VMEM)
 ANYWHERE = pl.BlockSpec(memory_space=pl.ANY)
 IN_HBM = pl.BlockSpec(memory_space=pltpu.HBM)
-SHARES = ([5, 5, 5, 5], 2, 2)
+SHARES = ([11, 11, 18], 4, 4)
 COLS = 1024
+EARLY = 192
 
 
 def in_vmem(array):
@@ -35,13 +36,20 @@
         self.packed = (self.full, width + (self.chunk if self.rest else 0))
 
 
-def pack_kernel(packing, first_hbm, second_hbm, out_ref, first_ref, second_ref, sems):
+def is_early():
+    return jnp.logical_and(lax.axis_index("sup") == 0, lax.axis_index("row") == 0)
+
+
+def pack_kernel(packing, low, first_hbm, second_hbm, schur_hbm, out_ref, room_ref, first_ref, second_ref, sems):
     copies = [
         pltpu.make_async_copy(first_hbm, first_ref, sems.at[0]),
         pltpu.make_async_copy(second_hbm, second_ref, sems.at[1]),
     ]
     for copy in copies:
         copy.start()
+    rows = min(EARLY, room_ref.shape[0])
+    ahead = pltpu.make_async_copy(schur_hbm.at[pl.ds(low, rows), :], room_ref.at[pl.ds(0, rows), :], sems.at[2])
+    pl.when(is_early())(ahead.start)
     for copy in copies:
         copy.wait()
     both = jnp.concatenate([first_ref[...], second_ref[...]], axis=0)
@@ -49,22 +57,23 @@
     for i in range(packing.fold if packing.rest else 0):
         lanes = slice(i * packing.chunk, (i + 1) * packing.chunk)
         out_ref[i * packing.rest : (i + 1) * packing.rest, packing.width :] = both[packing.full :, lanes]
-
-
-def pack(packing, first, second):
-    return pl.pallas_call(
-        functools.partial(pack_kernel, packing),
-        in_specs=[IN_HBM] * 2,
-        out_specs=WHOLE,
-        out_shape=pltpu.VMEM(packing.packed, first.dtype),
+    pl.when(is_early())(ahead.wait)
+
+
+def pack(packing, first, second, schur, low, rows):
+    return pl.pallas_call(
+        functools.partial(pack_kernel, packing, low),
+        in_specs=[IN_HBM] * 3,
+        out_specs=(WHOLE, WHOLE),
+        out_shape=(pltpu.VMEM(packing.packed, first.dtype), pltpu.VMEM((rows, schur.shape[1]), schur.dtype)),
         scratch_shapes=[
             pltpu.VMEM(first.shape, first.dtype),
             pltpu.VMEM(second.shape, second.dtype),
-            pltpu.SemaphoreType.DMA((2,)),
+            pltpu.SemaphoreType.DMA((3,)),
         ],
         compiler_params=pltpu.CompilerParams(vmem_limit_bytes=8 * MIB),
         name="pack",
-    )(in_hbm(first), in_hbm(second))
+    )(in_hbm(first), in_hbm(second), in_hbm(schur))
 
 
 def fetch_kernel(low, schur_ref, token_ref, out_ref, sem):
@@ -87,18 +96,74 @@
     )(in_hbm(schur), token)
 
 
+def fill_kernel(low, schur_ref, token_ref, room_ref, out_ref, sem):
+    rows = out_ref.shape[0]
+    skip = min(EARLY, rows)
+
+    def run(done):
+        copy = pltpu.make_async_copy(
+            schur_ref.at[pl.ds(low + done, rows - done), :], out_ref.at[pl.ds(done, rows - done), :], sem
+        )
+        copy.start()
+        copy.wait()
+
+    if rows > skip:
+        pl.when(is_early())(functools.partial(run, skip))
+    pl.when(jnp.logical_not(is_early()))(functools.partial(run, 0))
+
+
+def fill(schur, low, room, token):
+    rows, width = room.shape
+    return pl.pallas_call(
+        functools.partial(fill_kernel, low),
+        in_specs=[IN_HBM, ANYWHERE, WHOLE],
+        out_specs=WHOLE,
+        out_shape=pltpu.VMEM(room.shape, room.dtype),
+        input_output_aliases={2: 0},
+        scratch_shapes=[pltpu.SemaphoreType.DMA],
+        cost_estimate=pl.CostEstimate(flops=0, transcendentals=0, bytes_accessed=8 * rows * width),
+        compiler_params=pltpu.CompilerParams(vmem_limit_bytes=MIB),
+        name="fill",
+    )(in_hbm(schur), token, in_vmem(room))
+
+
 def shares_of(rows, hops):
     by_hop, by_swap, late = SHARES
     unit = rows // (sum(by_hop) + by_swap + late)
-    if hops != len(by_hop) or unit % 16 or unit * (sum(by_hop) + by_swap + late) != rows:
+    if hops != 4 or unit % 16 or unit * (sum(by_hop) + by_swap + late) != rows:
         return [], rows
     return [s * unit for s in by_hop], by_swap * unit
 
 
-def gather_rows(block, axis, schur, sizes):
+def pick_kernel(count, ahead_ref, behind_ref, out_ref):
+    index = lax.axis_index("row")
+    end = (index >= count // 2) == (index % 2 == 1)
+
+    @pl.when(end)
+    def _():
+        out_ref[...] = behind_ref[...]
+
+    @pl.when(jnp.logical_not(end))
+    def _():
+        out_ref[...] = ahead_ref[...]
+
+
+def pick(count, ahead, behind):
+    return pl.pallas_call(
+        functools.partial(pick_kernel, count),
+        in_specs=[WHOLE] * 2,
+        out_specs=WHOLE,
+        out_shape=pltpu.VMEM(ahead.shape, ahead.dtype),
+        compiler_params=pltpu.CompilerParams(vmem_limit_bytes=MIB),
+        name="pick",
+    )(in_vmem(ahead), in_vmem(behind))
+
+
+def gather_rows(block, axis, schur, room, sizes):
     count = lax.axis_size(axis)
     if not sizes:
         return [lax.all_gather(block, axis, axis=0)], []
+    assert count == 8
     ring = [2 * i for i in range(count // 2)] + [2 * i + 1 for i in reversed(range(count // 2))]
     place = {index: position for position, index in enumerate(ring)}
 
@@ -106,17 +171,18 @@
         return lax.ppermute(array, axis, [(i, ring[(place[i] + by) % count]) for i in range(count)])
 
     blocks, ahead, behind, fetched = [block], block, block, []
-    for hop in range(count // 2):
-        part = fetch(schur, sum(sizes[:hop]), sizes[hop], ahead)
-        ahead = step(ahead, 1)
-        if hop < count // 2 - 1:
-            behind = step(behind, -1)
+    for hop in range(3):
+        low = sum(sizes[:hop])
+        part = fetch(schur, low, sizes[hop], ahead) if hop < 2 else fill(schur, low, room, ahead)
+        if hop == 2:
+            across = pick(count, ahead, behind)
+            pairs = [(position, (position + 2) % count) for position in (2, 3, 6, 7)]
+            pairs += [(b, a) for a, b in pairs]
+            blocks.append(lax.ppermute(across, axis, [(ring[a], ring[b]) for a, b in pairs]))
+        ahead, behind = step(ahead, 1), step(behind, -1)
         ahead, part = lax.optimization_barrier((ahead, part))
-        if hop < count // 2 - 1:
-            behind, part = lax.optimization_barrier((behind, part))
-        blocks.append(ahead)
-        if hop < count // 2 - 1:
-            blocks.append(behind)
+        behind, part = lax.optimization_barrier((behind, part))
+        blocks += [ahead, behind]
         fetched.append(part)
     return [b[None] for b in blocks], fetched
 
@@ -243,7 +309,8 @@
     per_column = row_count // col_count
     packing = Packing(w_first.shape[0] + w_second.shape[0], width)
     sizes, beside_swap = shares_of(tile, row_count // 2)
-    pieces, parts = gather_rows(pack(packing, w_first, w_second), "row", schur_block, sizes)
+    packed, room = pack(packing, w_first, w_second, schur_block, sum(sizes[:-1]), sizes[-1] if sizes else 8)
+    pieces, parts = gather_rows(packed, "row", schur_block, room, sizes)
     build = assemble if tile % 128 == 0 else assemble_plain
     right, own = build(packing, pieces, tile, per_column)
     if beside_swap:

time: 38.8 us -> 37.9 us (0.977)
  the two profiles are of different devices: /device:TPU:1 before, /device:TPU:5 now
where the time goes in v3:
time: 37.9 us; the launch traced here: 37.6 us
  Pallas kernels  27.9 us (74%)
  starting transfers between devices  9.55 us (25%)
    pallas_call x1, Pallas kernels, update(): pl.pallas_call(functools.partial(update_kernel, columns, per_column), in_...  12.9 us
    pallas_call x3, Pallas kernels, fetch(): pl.pallas_call(functools.partial(fetch_kernel, low), in_specs=[IN_HBM, AN...  8.82 us
    pallas_call x1, Pallas kernels, fill(): pl.pallas_call(functools.partial(fill_kernel, low), in_specs=[IN_HBM, ANY...  5.03 us
    ppermute x6, starting transfers between devices, step(): lax.ppermute(array, axis, [(i, ring[(place[i] + by) % count]) for i in ra...  4.55 us
    ppermute x1, starting transfers between devices, per_device(): lax.ppermute(own, 'col', [(c, (c + 1) % col_count) for c in range(col_cou...  2.7 us
    ppermute x1, starting transfers between devices, gather_rows(): lax.ppermute(across, axis, [(ring[a], ring[b]) for a, b in pairs])  2.29 us
    pallas_call x1, Pallas kernels, pack(): pl.pallas_call(functools.partial(pack_kernel, packing, low), in_specs=[IN...  1.03 us
  transfers between devices with their start and end apart: 8, of which 0 were waited for; matrix products, arithmetic and copies ran while one was open for 0% of the time, Pallas kernels for 37%

profile of v3, /device:TPU:5, one launch (start us, length us, event | category | flops | bytes accessed | tf_op | source)
XLA Modules:
  0.0 37.6 jit_solution(9653801598173017800)
XLA Ops:
  0.0 1.0 %pack.1 = (bf16[8,7680]{1,0:T(8,128)(2,1)S(1)}, f32[576,6144]{1,0:T(8,128)S(1)}) custom-call(bf16[5,6144]{1,0:T(8,128)(2,1)} %first_hbm.1, bf16[5,6144]{1,0:T(8,128)(2,1)} %second_hbm.1, f32[1536,6144]{1,0:T(8,128)} %schur_hbm.3), custom_call_target="tpu_custom_call" | custom-call | tf_op jit(solution)/shard_map/pack/pallas_call | solution.py:64
  1.0 1.3 %collective-permute-start = (bf16[8,7680]{1,0:T(8,128)(2,1)S(1)}, bf16[8,7680]{1,0:T(8,128)(2,1)S(1)}, u32[]{:S(2)}, u32[]{:S(2)}) collective-permute-start(bf16[8,7680]{1,0:T(8,128)(2,1)S(1)} %get-tuple-element.22.token_ref), channel_id=1, source_target_pairs={{0,4},{2,0},{4,8},{6,2},{8,12},{10,6},{12,14},{14,10},{1,5},{3,1},... | collective-permute-start | bytes 368648 | tf_op jit(solution)/shard_map/ppermute | solution.py:171
  2.4 0.2 collective-permute-start.1
  2.6 3.5 %fetch.3.refs_0_ = f32[352,6144]{1,0:T(8,128)S(1)} custom-call(f32[1536,6144]{1,0:T(8,128)} %schur_hbm.3, bf16[8,7680]{1,0:T(8,128)(2,1)S(1)} %get-tuple-element.22.token_ref), custom_call_target="tpu_custom_call" | custom-call | bytes 17301504 | tf_op jit(solution)/shard_map/fetch/pallas_call | solution.py:87
  6.0 0.0 collective-permute-done.token_ref
  6.0 1.3 %collective-permute-start.2 = (bf16[8,7680]{1,0:T(8,128)(2,1)S(1)}, bf16[8,7680]{1,0:T(8,128)(2,1)S(1)}, u32[]{:S(2)}, u32[]{:S(2)}) collective-permute-start(bf16[8,7680]{1,0:T(8,128)(2,1)S(1)} %collective-permute-done.token_ref), channel_id=1, source_target_pairs={{0,4},{2,0},{4,8},{6,2},{8,12},{10,6},{12,14},{14,10},{1,5},{3,1},... | collective-permute-start | bytes 368648 | tf_op jit(solution)/shard_map/ppermute | solution.py:171
  7.4 0.0 collective-permute-done.1
  7.4 0.2 collective-permute-start.3
  7.6 3.5 %fetch.4.refs_1_ = f32[352,6144]{1,0:T(8,128)S(1)} custom-call(f32[1536,6144]{1,0:T(8,128)} %schur_hbm.3, bf16[8,7680]{1,0:T(8,128)(2,1)S(1)} %collective-permute-done.token_ref), custom_call_target="tpu_custom_call" | custom-call | bytes 17301504 | tf_op jit(solution)/shard_map/fetch/pallas_call | solution.py:87
  11.0 0.0 collective-permute-done.2.ahead_ref.token_ref
  11.0 1.3 %collective-permute-start.5 = (bf16[8,7680]{1,0:T(8,128)(2,1)S(1)}, bf16[8,7680]{1,0:T(8,128)(2,1)S(1)}, u32[]{:S(2)}, u32[]{:S(2)}) collective-permute-start(bf16[8,7680]{1,0:T(8,128)(2,1)S(1)} %collective-permute-done.2.ahead_ref.token_ref), channel_id=1, source_target_pairs={{0,4},{2,0},{4,8},{6,2},{8,12},{10,6},{12,14},{14,10},{1,5},{3,1},... | collective-permute-start | bytes 368648 | tf_op jit(solution)/shard_map/ppermute | solution.py:171
  12.4 0.0 collective-permute-done.3.behind_ref
  12.4 0.2 collective-permute-start.6
  12.6 2.3 %collective-permute-start.4 = (bf16[8,7680]{1,0:T(8,128)(2,1)S(1)}, bf16[8,7680]{1,0:T(8,128)(2,1)S(1)}, u32[]{:S(2)}, u32[]{:S(2)}) collective-permute-start(bf16[8,7680]{1,0:T(8,128)(2,1)S(1)} %pick.1), channel_id=1, source_target_pairs={{8,14},{12,10},{6,0},{2,4},{14,8},{10,12},{0,6},{4,2},{9,15},{13,1... | collective-permute-start | bytes 368648 | tf_op jit(solution)/shard_map/ppermute | solution.py:181
  14.9 5.0 %fill.1.refs_2_ = f32[576,6144]{1,0:T(8,128)S(1)} custom-call(f32[1536,6144]{1,0:T(8,128)} %schur_hbm.3, bf16[8,7680]{1,0:T(8,128)(2,1)S(1)} %collective-permute-done.2.ahead_ref.token_ref, f32[576,6144]{1,0:T(8,128)S(1)} %get-tuple-element.29.room_ref), custom_call_target="tpu_custom_call", output_to_operand_aliasing={{}: (2, {})} | custom-call | bytes 28311552 | tf_op jit(solution)/shard_map/fill/pallas_call | solution.py:117
  19.9 0.0 collective-permute-done.5
  19.9 0.0 collective-permute-done.6
  19.9 0.0 collective-permute-done.4
  19.9 0.1 assemble.1
  20.1 2.7 %collective-permute-start.7 = (bf16[80,1536]{1,0:T(8,128)(2,1)S(1)}, bf16[80,1536]{1,0:T(8,128)(2,1)S(1)}, u32[]{:S(2)}, u32[]{:S(2)}) collective-permute-start(bf16[80,1536]{1,0:T(8,128)(2,1)S(1)} %get-tuple-element.33.token_ref.own_ref), channel_id=1, source_target_pairs={{0,1},{1,0},{2,3},{3,2},{4,5},{5,4},{6,7},{7,6},{8,9},{9,8},{10,11... | collective-permute-start | bytes 737288 | tf_op jit(solution)/shard_map/ppermute | solution.py:318
  22.8 1.9 %fetch.5.refs_3_ = f32[128,6144]{1,0:T(8,128)S(1)} custom-call(f32[1536,6144]{1,0:T(8,128)} %schur_hbm.3, bf16[80,1536]{1,0:T(8,128)(2,1)S(1)} %get-tuple-element.33.token_ref.own_ref), custom_call_target="tpu_custom_call" | custom-call | bytes 6291456 | tf_op jit(solution)/shard_map/fetch/pallas_call | solution.py:87
  24.7 0.0 collective-permute-done.7.peer_ref
  24.7 12.9 %update.1 = (f32[1536,6144]{1,0:T(8,128)}, f32[352,6144]{1,0:T(8,128)S(1)}, f32[352,6144]{1,0:T(8,128)S(1)}, f32[576,6144]{1,0:T(8,128)S(1)}, f32[128,6144]{1,0:T(8,128)S(1)}) custom-call(f32[1536,6144]{1,0:T(8,128)} %schur_hbm.3, ...), custom_call_target="tpu_custom_call", output_to_operand_aliasing={{1}: (4, {}), {2}: (5, {}), {3}: (6, {}), {4}: (7, {})} | custom-call | tf_op jit(solution)/shard_map/update/pallas_call | solution.py:287
  (1 shorter events, 0.0 us)
Async XLA Ops:
  1.0 5.0 %collective-permute-start = (bf16[8,7680]{1,0:T(8,128)(2,1)S(1)}, bf16[8,7680]{1,0:T(8,128)(2,1)S(1)}, u32[]{:S(2)}, u32[]{:S(2)}) collective-permute-start(bf16[8,7680]{1,0:T(8,128)(2,1)S(1)} %get-tuple-element.22.token_ref), channel_id=1, source_target_pairs={{0,4},{2,0},{4,8},{6,2},{8,12},{10,6},{12,14},{14,10},{1,5},{3,1},... | collective-permute-start | bytes 368648 | tf_op jit(solution)/shard_map/ppermute | solution.py:171
  2.4 5.0 %collective-permute-start.1 = (bf16[8,7680]{1,0:T(8,128)(2,1)S(1)}, bf16[8,7680]{1,0:T(8,128)(2,1)S(1)}, u32[]{:S(2)}, u32[]{:S(2)}) collective-permute-start(bf16[8,7680]{1,0:T(8,128)(2,1)S(1)} %get-tuple-element.22.token_ref), channel_id=1, source_target_pairs={{0,2},{2,6},{4,0},{6,10},{8,4},{10,14},{12,8},{14,12},{1,3},{3,7},... | collective-permute-start | bytes 368648 | tf_op jit(solution)/shard_map/ppermute | solution.py:171
  6.0 5.0 %collective-permute-start.2 = (bf16[8,7680]{1,0:T(8,128)(2,1)S(1)}, bf16[8,7680]{1,0:T(8,128)(2,1)S(1)}, u32[]{:S(2)}, u32[]{:S(2)}) collective-permute-start(bf16[8,7680]{1,0:T(8,128)(2,1)S(1)} %collective-permute-done.token_ref), channel_id=1, source_target_pairs={{0,4},{2,0},{4,8},{6,2},{8,12},{10,6},{12,14},{14,10},{1,5},{3,1},... | collective-permute-start | bytes 368648 | tf_op jit(solution)/shard_map/ppermute | solution.py:171
  7.4 5.0 %collective-permute-start.3 = (bf16[8,7680]{1,0:T(8,128)(2,1)S(1)}, bf16[8,7680]{1,0:T(8,128)(2,1)S(1)}, u32[]{:S(2)}, u32[]{:S(2)}) collective-permute-start(bf16[8,7680]{1,0:T(8,128)(2,1)S(1)} %collective-permute-done.1), channel_id=1, source_target_pairs={{0,2},{2,6},{4,0},{6,10},{8,4},{10,14},{12,8},{14,12},{1,3},{3,7},... | collective-permute-start | bytes 368648 | tf_op jit(solution)/shard_map/ppermute | solution.py:171
  11.0 8.9 %collective-permute-start.5 = (bf16[8,7680]{1,0:T(8,128)(2,1)S(1)}, bf16[8,7680]{1,0:T(8,128)(2,1)S(1)}, u32[]{:S(2)}, u32[]{:S(2)}) collective-permute-start(bf16[8,7680]{1,0:T(8,128)(2,1)S(1)} %collective-permute-done.2.ahead_ref.token_ref), channel_id=1, source_target_pairs={{0,4},{2,0},{4,8},{6,2},{8,12},{10,6},{12,14},{14,10},{1,5},{3,1},... | collective-permute-start | bytes 368648 | tf_op jit(solution)/shard_map/ppermute | solution.py:171
  12.4 7.5 %collective-permute-start.6 = (bf16[8,7680]{1,0:T(8,128)(2,1)S(1)}, bf16[8,7680]{1,0:T(8,128)(2,1)S(1)}, u32[]{:S(2)}, u32[]{:S(2)}) collective-permute-start(bf16[8,7680]{1,0:T(8,128)(2,1)S(1)} %collective-permute-done.3.behind_ref), channel_id=1, source_target_pairs={{0,2},{2,6},{4,0},{6,10},{8,4},{10,14},{12,8},{14,12},{1,3},{3,7},... | collective-permute-start | bytes 368648 | tf_op jit(solution)/shard_map/ppermute | solution.py:171
  12.6 7.4 %collective-permute-start.4 = (bf16[8,7680]{1,0:T(8,128)(2,1)S(1)}, bf16[8,7680]{1,0:T(8,128)(2,1)S(1)}, u32[]{:S(2)}, u32[]{:S(2)}) collective-permute-start(bf16[8,7680]{1,0:T(8,128)(2,1)S(1)} %pick.1), channel_id=1, source_target_pairs={{8,14},{12,10},{6,0},{2,4},{14,8},{10,12},{0,6},{4,2},{9,15},{13,1... | collective-permute-start | bytes 368648 | tf_op jit(solution)/shard_map/ppermute | solution.py:181
  20.1 4.6 %collective-permute-start.7 = (bf16[80,1536]{1,0:T(8,128)(2,1)S(1)}, bf16[80,1536]{1,0:T(8,128)(2,1)S(1)}, u32[]{:S(2)}, u32[]{:S(2)}) collective-permute-start(bf16[80,1536]{1,0:T(8,128)(2,1)S(1)} %get-tuple-element.33.token_ref.own_ref), channel_id=1, source_target_pairs={{0,1},{1,0},{2,3},{3,2},{4,5},{5,4},{6,7},{7,6},{8,9},{9,8},{10,11... | collective-permute-start | bytes 737288 | tf_op jit(solution)/shard_map/ppermute | solution.py:318

commit v4 on v3

--- a/solution.py
+++ b/solution.py
@@ -13,7 +13,7 @@
 IN_HBM = pl.BlockSpec(memory_space=pltpu.HBM)
 SHARES = ([11, 11, 18], 4, 4)
 COLS = 1024
-EARLY = 192
+EARLY = 128
 
 
 def in_vmem(array):
@@ -40,18 +40,10 @@
     return jnp.logical_and(lax.axis_index("sup") == 0, lax.axis_index("row") == 0)
 
 
-def pack_kernel(packing, low, first_hbm, second_hbm, schur_hbm, out_ref, room_ref, first_ref, second_ref, sems):
-    copies = [
-        pltpu.make_async_copy(first_hbm, first_ref, sems.at[0]),
-        pltpu.make_async_copy(second_hbm, second_ref, sems.at[1]),
-    ]
-    for copy in copies:
-        copy.start()
+def pack_kernel(packing, low, first_ref, second_ref, schur_hbm, out_ref, room_ref, sem):
     rows = min(EARLY, room_ref.shape[0])
-    ahead = pltpu.make_async_copy(schur_hbm.at[pl.ds(low, rows), :], room_ref.at[pl.ds(0, rows), :], sems.at[2])
+    ahead = pltpu.make_async_copy(schur_hbm.at[pl.ds(low, rows), :], room_ref.at[pl.ds(0, rows), :], sem)
     pl.when(is_early())(ahead.start)
-    for copy in copies:
-        copy.wait()
     both = jnp.concatenate([first_ref[...], second_ref[...]], axis=0)
     out_ref[:, : packing.width] = both[: packing.full]
     for i in range(packing.fold if packing.rest else 0):
@@ -63,14 +55,10 @@
 def pack(packing, first, second, schur, low, rows):
     return pl.pallas_call(
         functools.partial(pack_kernel, packing, low),
-        in_specs=[IN_HBM] * 3,
+        in_specs=[WHOLE, WHOLE, IN_HBM],
         out_specs=(WHOLE, WHOLE),
         out_shape=(pltpu.VMEM(packing.packed, first.dtype), pltpu.VMEM((rows, schur.shape[1]), schur.dtype)),
-        scratch_shapes=[
-            pltpu.VMEM(first.shape, first.dtype),
-            pltpu.VMEM(second.shape, second.dtype),
-            pltpu.SemaphoreType.DMA((3,)),
-        ],
+        scratch_shapes=[pltpu.SemaphoreType.DMA],
         compiler_params=pltpu.CompilerParams(vmem_limit_bytes=8 * MIB),
         name="pack",
     )(in_hbm(first), in_hbm(second), in_hbm(schur))

time: 37.9 us -> 37.9 us (level)
  the two profiles are of different devices: /device:TPU:5 before, /device:TPU:1 now
where the time goes in v4:
time: 37.9 us; the launch traced here: 37.5 us
  Pallas kernels  28.8 us (76%)
  starting transfers between devices  8.27 us (22%)
    pallas_call x1, Pallas kernels, update(): pl.pallas_call(functools.partial(update_kernel, columns, per_column), in_...  12.9 us
    pallas_call x3, Pallas kernels, fetch(): pl.pallas_call(functools.partial(fetch_kernel, low), in_specs=[IN_HBM, AN...  8.82 us
    ppermute x6, starting transfers between devices, step(): lax.ppermute(array, axis, [(i, ring[(place[i] + by) % count]) for i in ra...  4.55 us
    pallas_call x1, Pallas kernels, fill(): pl.pallas_call(functools.partial(fill_kernel, low), in_specs=[IN_HBM, ANY...  4.14 us
    pallas_call x1, Pallas kernels, pack(): pl.pallas_call(functools.partial(pack_kernel, packing, low), in_specs=[WH...  2.85 us
    ppermute x1, starting transfers between devices, per_device(): lax.ppermute(own, 'col', [(c, (c + 1) % col_count) for c in range(col_cou...  2.43 us
    ppermute x1, starting transfers between devices, gather_rows(): lax.ppermute(across, axis, [(ring[a], ring[b]) for a, b in pairs])  1.28 us
  transfers between devices with their start and end apart: 8, of which 1 were waited for; matrix products, arithmetic and copies ran while one was open for 0% of the time, Pallas kernels for 35%

profile of v4, /device:TPU:1, one launch (start us, length us, event | category | flops | bytes accessed | tf_op | source)
XLA Modules:
  0.0 37.5 jit_solution(114597642658508135)
XLA Ops:
  0.0 2.8 %pack.1 = (bf16[8,7680]{1,0:T(8,128)(2,1)S(1)}, f32[576,6144]{1,0:T(8,128)S(1)}) custom-call(bf16[5,6144]{1,0:T(8,128)(2,1)} %first_ref.1, bf16[5,6144]{1,0:T(8,128)(2,1)} %second_ref.1, f32[1536,6144]{1,0:T(8,128)} %schur_hbm.3), custom_call_target="tpu_custom_call" | custom-call | tf_op jit(solution)/shard_map/pack/pallas_call | solution.py:56
  2.9 0.3 collective-permute-start
  3.2 1.2 %collective-permute-start.1 = (bf16[8,7680]{1,0:T(8,128)(2,1)S(1)}, bf16[8,7680]{1,0:T(8,128)(2,1)S(1)}, u32[]{:S(2)}, u32[]{:S(2)}) collective-permute-start(bf16[8,7680]{1,0:T(8,128)(2,1)S(1)} %get-tuple-element.22.token_ref), channel_id=1, source_target_pairs={{0,2},{2,6},{4,0},{6,10},{8,4},{10,14},{12,8},{14,12},{1,3},{3,7},... | collective-permute-start | bytes 368648 | tf_op jit(solution)/shard_map/ppermute | solution.py:159
  4.4 3.5 %fetch.3.refs_0_ = f32[352,6144]{1,0:T(8,128)S(1)} custom-call(f32[1536,6144]{1,0:T(8,128)} %schur_hbm.3, bf16[8,7680]{1,0:T(8,128)(2,1)S(1)} %get-tuple-element.22.token_ref), custom_call_target="tpu_custom_call" | custom-call | bytes 17301504 | tf_op jit(solution)/shard_map/fetch/pallas_call | solution.py:75
  7.8 0.0 collective-permute-done.token_ref
  7.9 0.3 collective-permute-start.2
  8.2 0.0 collective-permute-done.1
  8.2 1.2 %collective-permute-start.3 = (bf16[8,7680]{1,0:T(8,128)(2,1)S(1)}, bf16[8,7680]{1,0:T(8,128)(2,1)S(1)}, u32[]{:S(2)}, u32[]{:S(2)}) collective-permute-start(bf16[8,7680]{1,0:T(8,128)(2,1)S(1)} %collective-permute-done.1), channel_id=1, source_target_pairs={{0,2},{2,6},{4,0},{6,10},{8,4},{10,14},{12,8},{14,12},{1,3},{3,7},... | collective-permute-start | bytes 368648 | tf_op jit(solution)/shard_map/ppermute | solution.py:159
  9.4 3.5 %fetch.4.refs_1_ = f32[352,6144]{1,0:T(8,128)S(1)} custom-call(f32[1536,6144]{1,0:T(8,128)} %schur_hbm.3, bf16[8,7680]{1,0:T(8,128)(2,1)S(1)} %collective-permute-done.token_ref), custom_call_target="tpu_custom_call" | custom-call | bytes 17301504 | tf_op jit(solution)/shard_map/fetch/pallas_call | solution.py:75
  12.9 0.0 collective-permute-done.2.ahead_ref.token_ref
  12.9 0.3 collective-permute-start.5
  13.2 0.0 collective-permute-done.3.behind_ref
  13.2 1.2 %collective-permute-start.6 = (bf16[8,7680]{1,0:T(8,128)(2,1)S(1)}, bf16[8,7680]{1,0:T(8,128)(2,1)S(1)}, u32[]{:S(2)}, u32[]{:S(2)}) collective-permute-start(bf16[8,7680]{1,0:T(8,128)(2,1)S(1)} %collective-permute-done.3.behind_ref), channel_id=1, source_target_pairs={{0,2},{2,6},{4,0},{6,10},{8,4},{10,14},{12,8},{14,12},{1,3},{3,7},... | collective-permute-start | bytes 368648 | tf_op jit(solution)/shard_map/ppermute | solution.py:159
  14.4 1.3 %collective-permute-start.4 = (bf16[8,7680]{1,0:T(8,128)(2,1)S(1)}, bf16[8,7680]{1,0:T(8,128)(2,1)S(1)}, u32[]{:S(2)}, u32[]{:S(2)}) collective-permute-start(bf16[8,7680]{1,0:T(8,128)(2,1)S(1)} %pick.1), channel_id=1, source_target_pairs={{8,14},{12,10},{6,0},{2,4},{14,8},{10,12},{0,6},{4,2},{9,15},{13,1... | collective-permute-start | bytes 368648 | tf_op jit(solution)/shard_map/ppermute | solution.py:169
  15.7 4.1 %fill.1.refs_2_ = f32[576,6144]{1,0:T(8,128)S(1)} custom-call(f32[1536,6144]{1,0:T(8,128)} %schur_hbm.3, bf16[8,7680]{1,0:T(8,128)(2,1)S(1)} %collective-permute-done.2.ahead_ref.token_ref, f32[576,6144]{1,0:T(8,128)S(1)} %get-tuple-element.29.room_ref), custom_call_target="tpu_custom_call", output_to_operand_aliasing={{}: (2, {})} | custom-call | bytes 28311552 | tf_op jit(solution)/shard_map/fill/pallas_call | solution.py:105
  19.8 0.0 collective-permute-done.5
  19.8 0.0 collective-permute-done.6
  19.8 0.3 collective-permute-done.4
  20.1 0.1 assemble.1
  20.3 2.4 %collective-permute-start.7 = (bf16[80,1536]{1,0:T(8,128)(2,1)S(1)}, bf16[80,1536]{1,0:T(8,128)(2,1)S(1)}, u32[]{:S(2)}, u32[]{:S(2)}) collective-permute-start(bf16[80,1536]{1,0:T(8,128)(2,1)S(1)} %get-tuple-element.33.token_ref.own_ref), channel_id=1, source_target_pairs={{0,1},{1,0},{2,3},{3,2},{4,5},{5,4},{6,7},{7,6},{8,9},{9,8},{10,11... | collective-permute-start | bytes 737288 | tf_op jit(solution)/shard_map/ppermute | solution.py:306
  22.7 1.9 %fetch.5.refs_3_ = f32[128,6144]{1,0:T(8,128)S(1)} custom-call(f32[1536,6144]{1,0:T(8,128)} %schur_hbm.3, bf16[80,1536]{1,0:T(8,128)(2,1)S(1)} %get-tuple-element.33.token_ref.own_ref), custom_call_target="tpu_custom_call" | custom-call | bytes 6291456 | tf_op jit(solution)/shard_map/fetch/pallas_call | solution.py:75
  24.6 0.0 collective-permute-done.7.peer_ref
  24.6 12.9 %update.1 = (f32[1536,6144]{1,0:T(8,128)}, f32[352,6144]{1,0:T(8,128)S(1)}, f32[352,6144]{1,0:T(8,128)S(1)}, f32[576,6144]{1,0:T(8,128)S(1)}, f32[128,6144]{1,0:T(8,128)S(1)}) custom-call(f32[1536,6144]{1,0:T(8,128)} %schur_hbm.3, ...), custom_call_target="tpu_custom_call", output_to_operand_aliasing={{1}: (4, {}), {2}: (5, {}), {3}: (6, {}), {4}: (7, {})} | custom-call | tf_op jit(solution)/shard_map/update/pallas_call | solution.py:275
  (1 shorter events, 0.0 us)
Async XLA Ops:
  2.9 5.0 %collective-permute-start = (bf16[8,7680]{1,0:T(8,128)(2,1)S(1)}, bf16[8,7680]{1,0:T(8,128)(2,1)S(1)}, u32[]{:S(2)}, u32[]{:S(2)}) collective-permute-start(bf16[8,7680]{1,0:T(8,128)(2,1)S(1)} %get-tuple-element.22.token_ref), channel_id=1, source_target_pairs={{0,4},{2,0},{4,8},{6,2},{8,12},{10,6},{12,14},{14,10},{1,5},{3,1},... | collective-permute-start | bytes 368648 | tf_op jit(solution)/shard_map/ppermute | solution.py:159
  3.2 5.0 %collective-permute-start.1 = (bf16[8,7680]{1,0:T(8,128)(2,1)S(1)}, bf16[8,7680]{1,0:T(8,128)(2,1)S(1)}, u32[]{:S(2)}, u32[]{:S(2)}) collective-permute-start(bf16[8,7680]{1,0:T(8,128)(2,1)S(1)} %get-tuple-element.22.token_ref), channel_id=1, source_target_pairs={{0,2},{2,6},{4,0},{6,10},{8,4},{10,14},{12,8},{14,12},{1,3},{3,7},... | collective-permute-start | bytes 368648 | tf_op jit(solution)/shard_map/ppermute | solution.py:159
  7.9 5.0 %collective-permute-start.2 = (bf16[8,7680]{1,0:T(8,128)(2,1)S(1)}, bf16[8,7680]{1,0:T(8,128)(2,1)S(1)}, u32[]{:S(2)}, u32[]{:S(2)}) collective-permute-start(bf16[8,7680]{1,0:T(8,128)(2,1)S(1)} %collective-permute-done.token_ref), channel_id=1, source_target_pairs={{0,4},{2,0},{4,8},{6,2},{8,12},{10,6},{12,14},{14,10},{1,5},{3,1},... | collective-permute-start | bytes 368648 | tf_op jit(solution)/shard_map/ppermute | solution.py:159
  8.2 5.0 %collective-permute-start.3 = (bf16[8,7680]{1,0:T(8,128)(2,1)S(1)}, bf16[8,7680]{1,0:T(8,128)(2,1)S(1)}, u32[]{:S(2)}, u32[]{:S(2)}) collective-permute-start(bf16[8,7680]{1,0:T(8,128)(2,1)S(1)} %collective-permute-done.1), channel_id=1, source_target_pairs={{0,2},{2,6},{4,0},{6,10},{8,4},{10,14},{12,8},{14,12},{1,3},{3,7},... | collective-permute-start | bytes 368648 | tf_op jit(solution)/shard_map/ppermute | solution.py:159
  12.9 7.0 %collective-permute-start.5 = (bf16[8,7680]{1,0:T(8,128)(2,1)S(1)}, bf16[8,7680]{1,0:T(8,128)(2,1)S(1)}, u32[]{:S(2)}, u32[]{:S(2)}) collective-permute-start(bf16[8,7680]{1,0:T(8,128)(2,1)S(1)} %collective-permute-done.2.ahead_ref.token_ref), channel_id=1, source_target_pairs={{0,4},{2,0},{4,8},{6,2},{8,12},{10,6},{12,14},{14,10},{1,5},{3,1},... | collective-permute-start | bytes 368648 | tf_op jit(solution)/shard_map/ppermute | solution.py:159
  13.2 6.6 %collective-permute-start.6 = (bf16[8,7680]{1,0:T(8,128)(2,1)S(1)}, bf16[8,7680]{1,0:T(8,128)(2,1)S(1)}, u32[]{:S(2)}, u32[]{:S(2)}) collective-permute-start(bf16[8,7680]{1,0:T(8,128)(2,1)S(1)} %collective-permute-done.3.behind_ref), channel_id=1, source_target_pairs={{0,2},{2,6},{4,0},{6,10},{8,4},{10,14},{12,8},{14,12},{1,3},{3,7},... | collective-permute-start | bytes 368648 | tf_op jit(solution)/shard_map/ppermute | solution.py:159
  14.4 5.7 %collective-permute-start.4 = (bf16[8,7680]{1,0:T(8,128)(2,1)S(1)}, bf16[8,7680]{1,0:T(8,128)(2,1)S(1)}, u32[]{:S(2)}, u32[]{:S(2)}) collective-permute-start(bf16[8,7680]{1,0:T(8,128)(2,1)S(1)} %pick.1), channel_id=1, source_target_pairs={{8,14},{12,10},{6,0},{2,4},{14,8},{10,12},{0,6},{4,2},{9,15},{13,1... | collective-permute-start | bytes 368648 | tf_op jit(solution)/shard_map/ppermute | solution.py:169
  20.3 4.3 %collective-permute-start.7 = (bf16[80,1536]{1,0:T(8,128)(2,1)S(1)}, bf16[80,1536]{1,0:T(8,128)(2,1)S(1)}, u32[]{:S(2)}, u32[]{:S(2)}) collective-permute-start(bf16[80,1536]{1,0:T(8,128)(2,1)S(1)} %get-tuple-element.33.token_ref.own_ref), channel_id=1, source_target_pairs={{0,1},{1,0},{2,3},{3,2},{4,5},{5,4},{6,7},{7,6},{8,9},{9,8},{10,11... | collective-permute-start | bytes 737288 | tf_op jit(solution)/shard_map/ppermute | solution.py:306

commit v5 on v4

--- a/solution.py
+++ b/solution.py
@@ -14,6 +14,7 @@
 SHARES = ([11, 11, 18], 4, 4)
 COLS = 1024
 EARLY = 128
+WAITING = 48
 
 
 def in_vmem(array):
@@ -86,7 +87,6 @@
 
 def fill_kernel(low, schur_ref, token_ref, room_ref, out_ref, sem):
     rows = out_ref.shape[0]
-    skip = min(EARLY, rows)
 
     def run(done):
         copy = pltpu.make_async_copy(
@@ -95,9 +95,10 @@
         copy.start()
         copy.wait()
 
-    if rows > skip:
-        pl.when(is_early())(functools.partial(run, skip))
-    pl.when(jnp.logical_not(is_early()))(functools.partial(run, 0))
+    early, waiting = is_early(), is_waiting()
+    pl.when(early)(functools.partial(run, EARLY))
+    pl.when(waiting)(functools.partial(run, WAITING))
+    pl.when(jnp.logical_not(jnp.logical_or(early, waiting)))(functools.partial(run, 0))
 
 
 def fill(schur, low, room, token):
@@ -120,12 +121,17 @@
     unit = rows // (sum(by_hop) + by_swap + late)
     if hops != 4 or unit % 16 or unit * (sum(by_hop) + by_swap + late) != rows:
         return [], rows
+    assert by_hop[-1] * unit > max(EARLY, WAITING)
     return [s * unit for s in by_hop], by_swap * unit
 
 
-def pick_kernel(count, ahead_ref, behind_ref, out_ref):
+def is_waiting():
+    return jnp.logical_and(lax.axis_index("row") % 4 == 0, jnp.logical_not(is_early()))
+
+
+def pick_kernel(low, ahead_ref, behind_ref, schur_ref, room_ref, out_ref, filled_ref, sem):
     index = lax.axis_index("row")
-    end = (index >= count // 2) == (index % 2 == 1)
+    end = (index >= lax.axis_size("row") // 2) == (index % 2 == 1)
 
     @pl.when(end)
     def _():
@@ -135,16 +141,26 @@
     def _():
         out_ref[...] = ahead_ref[...]
 
-
-def pick(count, ahead, behind):
-    return pl.pallas_call(
-        functools.partial(pick_kernel, count),
-        in_specs=[WHOLE] * 2,
-        out_specs=WHOLE,
-        out_shape=pltpu.VMEM(ahead.shape, ahead.dtype),
+    def run(done):
+        rows = pl.ds(done, WAITING)
+        copy = pltpu.make_async_copy(schur_ref.at[pl.ds(low + done, WAITING), :], filled_ref.at[rows, :], sem)
+        copy.start()
+        copy.wait()
+
+    pl.when(is_waiting())(functools.partial(run, 0))
+
+
+def pick(low, ahead, behind, schur, room):
+    return pl.pallas_call(
+        functools.partial(pick_kernel, low),
+        in_specs=[WHOLE, WHOLE, IN_HBM, WHOLE],
+        out_specs=(WHOLE, WHOLE),
+        out_shape=(pltpu.VMEM(ahead.shape, ahead.dtype), pltpu.VMEM(room.shape, room.dtype)),
+        input_output_aliases={3: 1},
+        scratch_shapes=[pltpu.SemaphoreType.DMA],
         compiler_params=pltpu.CompilerParams(vmem_limit_bytes=MIB),
         name="pick",
-    )(in_vmem(ahead), in_vmem(behind))
+    )(in_vmem(ahead), in_vmem(behind), in_hbm(schur), in_vmem(room))
 
 
 def gather_rows(block, axis, schur, room, sizes):
@@ -161,9 +177,11 @@
     blocks, ahead, behind, fetched = [block], block, block, []
     for hop in range(3):
         low = sum(sizes[:hop])
-        part = fetch(schur, low, sizes[hop], ahead) if hop < 2 else fill(schur, low, room, ahead)
-        if hop == 2:
-            across = pick(count, ahead, behind)
+        if hop < 2:
+            part = fetch(schur, low, sizes[hop], ahead)
+        else:
+            across, room = pick(low, ahead, behind, schur, room)
+            part = fill(schur, low, room, across)
             pairs = [(position, (position + 2) % count) for position in (2, 3, 6, 7)]
             pairs += [(b, a) for a, b in pairs]
             blocks.append(lax.ppermute(across, axis, [(ring[a], ring[b]) for a, b in pairs]))

time: 37.9 us -> 37.8 us (level)
  no operation moved by 1% of the time
where the time goes in v5:
time: 37.8 us; the launch traced here: 37.5 us
  Pallas kernels  28.8 us (76%)
  starting transfers between devices  8.28 us (22%)
    pallas_call x1, Pallas kernels, update(): pl.pallas_call(functools.partial(update_kernel, columns, per_column), in_...  12.9 us
    pallas_call x3, Pallas kernels, fetch(): pl.pallas_call(functools.partial(fetch_kernel, low), in_specs=[IN_HBM, AN...  8.82 us
    ppermute x6, starting transfers between devices, step(): lax.ppermute(array, axis, [(i, ring[(place[i] + by) % count]) for i in ra...  4.55 us
    pallas_call x1, Pallas kernels, fill(): pl.pallas_call(functools.partial(fill_kernel, low), in_specs=[IN_HBM, ANY...  4.14 us
    pallas_call x1, Pallas kernels, pack(): pl.pallas_call(functools.partial(pack_kernel, packing, low), in_specs=[WH...  2.85 us
    ppermute x1, starting transfers between devices, per_device(): lax.ppermute(own, 'col', [(c, (c + 1) % col_count) for c in range(col_cou...  2.45 us
    ppermute x1, starting transfers between devices, gather_rows(): lax.ppermute(across, axis, [(ring[a], ring[b]) for a, b in pairs])  1.28 us
  transfers between devices with their start and end apart: 8, of which 1 were waited for; matrix products, arithmetic and copies ran while one was open for 0% of the time, Pallas kernels for 35%

profile of v5, /device:TPU:1, one launch (start us, length us, event | category | flops | bytes accessed | tf_op | source)
XLA Modules:
  0.0 37.5 jit_solution(4085086478240407140)
XLA Ops:
  0.0 2.8 %pack.1 = (bf16[8,7680]{1,0:T(8,128)(2,1)S(1)}, f32[576,6144]{1,0:T(8,128)S(1)}) custom-call(bf16[5,6144]{1,0:T(8,128)(2,1)} %first_ref.1, bf16[5,6144]{1,0:T(8,128)(2,1)} %second_ref.1, f32[1536,6144]{1,0:T(8,128)} %schur_hbm.3), custom_call_target="tpu_custom_call" | custom-call | tf_op jit(solution)/shard_map/pack/pallas_call | solution.py:57
  2.9 0.3 collective-permute-start
  3.2 1.2 %collective-permute-start.1 = (bf16[8,7680]{1,0:T(8,128)(2,1)S(1)}, bf16[8,7680]{1,0:T(8,128)(2,1)S(1)}, u32[]{:S(2)}, u32[]{:S(2)}) collective-permute-start(bf16[8,7680]{1,0:T(8,128)(2,1)S(1)} %get-tuple-element.24.token_ref), channel_id=1, source_target_pairs={{0,2},{2,6},{4,0},{6,10},{8,4},{10,14},{12,8},{14,12},{1,3},{3,7},... | collective-permute-start | bytes 368648 | tf_op jit(solution)/shard_map/ppermute | solution.py:175
  4.4 3.5 %fetch.3.refs_0_ = f32[352,6144]{1,0:T(8,128)S(1)} custom-call(f32[1536,6144]{1,0:T(8,128)} %schur_hbm.3, bf16[8,7680]{1,0:T(8,128)(2,1)S(1)} %get-tuple-element.24.token_ref), custom_call_target="tpu_custom_call" | custom-call | bytes 17301504 | tf_op jit(solution)/shard_map/fetch/pallas_call | solution.py:76
  7.8 0.0 collective-permute-done.token_ref
  7.9 0.3 collective-permute-start.2
  8.2 0.0 collective-permute-done.1
  8.2 1.2 %collective-permute-start.3 = (bf16[8,7680]{1,0:T(8,128)(2,1)S(1)}, bf16[8,7680]{1,0:T(8,128)(2,1)S(1)}, u32[]{:S(2)}, u32[]{:S(2)}) collective-permute-start(bf16[8,7680]{1,0:T(8,128)(2,1)S(1)} %collective-permute-done.1), channel_id=1, source_target_pairs={{0,2},{2,6},{4,0},{6,10},{8,4},{10,14},{12,8},{14,12},{1,3},{3,7},... | collective-permute-start | bytes 368648 | tf_op jit(solution)/shard_map/ppermute | solution.py:175
  9.4 3.5 %fetch.4.refs_1_ = f32[352,6144]{1,0:T(8,128)S(1)} custom-call(f32[1536,6144]{1,0:T(8,128)} %schur_hbm.3, bf16[8,7680]{1,0:T(8,128)(2,1)S(1)} %collective-permute-done.token_ref), custom_call_target="tpu_custom_call" | custom-call | bytes 17301504 | tf_op jit(solution)/shard_map/fetch/pallas_call | solution.py:76
  12.9 0.0 collective-permute-done.2.ahead_ref
  12.9 0.3 collective-permute-start.5
  13.2 0.0 collective-permute-done.3.behind_ref
  13.2 1.2 %collective-permute-start.6 = (bf16[8,7680]{1,0:T(8,128)(2,1)S(1)}, bf16[8,7680]{1,0:T(8,128)(2,1)S(1)}, u32[]{:S(2)}, u32[]{:S(2)}) collective-permute-start(bf16[8,7680]{1,0:T(8,128)(2,1)S(1)} %collective-permute-done.3.behind_ref), channel_id=1, source_target_pairs={{0,2},{2,6},{4,0},{6,10},{8,4},{10,14},{12,8},{14,12},{1,3},{3,7},... | collective-permute-start | bytes 368648 | tf_op jit(solution)/shard_map/ppermute | solution.py:175
  14.4 1.3 %collective-permute-start.4 = (bf16[8,7680]{1,0:T(8,128)(2,1)S(1)}, bf16[8,7680]{1,0:T(8,128)(2,1)S(1)}, u32[]{:S(2)}, u32[]{:S(2)}) collective-permute-start(bf16[8,7680]{1,0:T(8,128)(2,1)S(1)} %get-tuple-element.32.token_ref), channel_id=1, source_target_pairs={{8,14},{12,10},{6,0},{2,4},{14,8},{10,12},{0,6},{4,2},{9,15},{13,1... | collective-permute-start | bytes 368648 | tf_op jit(solution)/shard_map/ppermute | solution.py:187
  15.7 4.1 %fill.1.refs_2_ = f32[576,6144]{1,0:T(8,128)S(1)} custom-call(f32[1536,6144]{1,0:T(8,128)} %schur_hbm.3, bf16[8,7680]{1,0:T(8,128)(2,1)S(1)} %get-tuple-element.32.token_ref, f32[576,6144]{1,0:T(8,128)S(1)} %get-tuple-element.33.room_ref), custom_call_target="tpu_custom_call", output_to_operand_aliasing={{}: (2, {})} | custom-call | bytes 28311552 | tf_op jit(solution)/shard_map/fill/pallas_call | solution.py:106
  19.8 0.0 collective-permute-done.5
  19.9 0.0 collective-permute-done.6
  19.9 0.3 collective-permute-done.4
  20.1 0.1 assemble.1
  20.3 2.4 %collective-permute-start.7 = (bf16[80,1536]{1,0:T(8,128)(2,1)S(1)}, bf16[80,1536]{1,0:T(8,128)(2,1)S(1)}, u32[]{:S(2)}, u32[]{:S(2)}) collective-permute-start(bf16[80,1536]{1,0:T(8,128)(2,1)S(1)} %get-tuple-element.37.token_ref.own_ref), channel_id=1, source_target_pairs={{0,1},{1,0},{2,3},{3,2},{4,5},{5,4},{6,7},{7,6},{8,9},{9,8},{10,11... | collective-permute-start | bytes 737288 | tf_op jit(solution)/shard_map/ppermute | solution.py:324
  22.7 1.9 %fetch.5.refs_3_ = f32[128,6144]{1,0:T(8,128)S(1)} custom-call(f32[1536,6144]{1,0:T(8,128)} %schur_hbm.3, bf16[80,1536]{1,0:T(8,128)(2,1)S(1)} %get-tuple-element.37.token_ref.own_ref), custom_call_target="tpu_custom_call" | custom-call | bytes 6291456 | tf_op jit(solution)/shard_map/fetch/pallas_call | solution.py:76
  24.6 0.0 collective-permute-done.7.peer_ref
  24.6 12.9 %update.1 = (f32[1536,6144]{1,0:T(8,128)}, f32[352,6144]{1,0:T(8,128)S(1)}, f32[352,6144]{1,0:T(8,128)S(1)}, f32[576,6144]{1,0:T(8,128)S(1)}, f32[128,6144]{1,0:T(8,128)S(1)}) custom-call(f32[1536,6144]{1,0:T(8,128)} %schur_hbm.3, ...), custom_call_target="tpu_custom_call", output_to_operand_aliasing={{1}: (4, {}), {2}: (5, {}), {3}: (6, {}), {4}: (7, {})} | custom-call | tf_op jit(solution)/shard_map/update/pallas_call | solution.py:293
  (1 shorter events, 0.0 us)
Async XLA Ops:
  2.9 5.0 %collective-permute-start = (bf16[8,7680]{1,0:T(8,128)(2,1)S(1)}, bf16[8,7680]{1,0:T(8,128)(2,1)S(1)}, u32[]{:S(2)}, u32[]{:S(2)}) collective-permute-start(bf16[8,7680]{1,0:T(8,128)(2,1)S(1)} %get-tuple-element.24.token_ref), channel_id=1, source_target_pairs={{0,4},{2,0},{4,8},{6,2},{8,12},{10,6},{12,14},{14,10},{1,5},{3,1},... | collective-permute-start | bytes 368648 | tf_op jit(solution)/shard_map/ppermute | solution.py:175
  3.2 5.0 %collective-permute-start.1 = (bf16[8,7680]{1,0:T(8,128)(2,1)S(1)}, bf16[8,7680]{1,0:T(8,128)(2,1)S(1)}, u32[]{:S(2)}, u32[]{:S(2)}) collective-permute-start(bf16[8,7680]{1,0:T(8,128)(2,1)S(1)} %get-tuple-element.24.token_ref), channel_id=1, source_target_pairs={{0,2},{2,6},{4,0},{6,10},{8,4},{10,14},{12,8},{14,12},{1,3},{3,7},... | collective-permute-start | bytes 368648 | tf_op jit(solution)/shard_map/ppermute | solution.py:175
  7.9 5.0 %collective-permute-start.2 = (bf16[8,7680]{1,0:T(8,128)(2,1)S(1)}, bf16[8,7680]{1,0:T(8,128)(2,1)S(1)}, u32[]{:S(2)}, u32[]{:S(2)}) collective-permute-start(bf16[8,7680]{1,0:T(8,128)(2,1)S(1)} %collective-permute-done.token_ref), channel_id=1, source_target_pairs={{0,4},{2,0},{4,8},{6,2},{8,12},{10,6},{12,14},{14,10},{1,5},{3,1},... | collective-permute-start | bytes 368648 | tf_op jit(solution)/shard_map/ppermute | solution.py:175
  8.2 5.0 %collective-permute-start.3 = (bf16[8,7680]{1,0:T(8,128)(2,1)S(1)}, bf16[8,7680]{1,0:T(8,128)(2,1)S(1)}, u32[]{:S(2)}, u32[]{:S(2)}) collective-permute-start(bf16[8,7680]{1,0:T(8,128)(2,1)S(1)} %collective-permute-done.1), channel_id=1, source_target_pairs={{0,2},{2,6},{4,0},{6,10},{8,4},{10,14},{12,8},{14,12},{1,3},{3,7},... | collective-permute-start | bytes 368648 | tf_op jit(solution)/shard_map/ppermute | solution.py:175
  12.9 7.0 %collective-permute-start.5 = (bf16[8,7680]{1,0:T(8,128)(2,1)S(1)}, bf16[8,7680]{1,0:T(8,128)(2,1)S(1)}, u32[]{:S(2)}, u32[]{:S(2)}) collective-permute-start(bf16[8,7680]{1,0:T(8,128)(2,1)S(1)} %collective-permute-done.2.ahead_ref), channel_id=1, source_target_pairs={{0,4},{2,0},{4,8},{6,2},{8,12},{10,6},{12,14},{14,10},{1,5},{3,1},... | collective-permute-start | bytes 368648 | tf_op jit(solution)/shard_map/ppermute | solution.py:175
  13.2 6.6 %collective-permute-start.6 = (bf16[8,7680]{1,0:T(8,128)(2,1)S(1)}, bf16[8,7680]{1,0:T(8,128)(2,1)S(1)}, u32[]{:S(2)}, u32[]{:S(2)}) collective-permute-start(bf16[8,7680]{1,0:T(8,128)(2,1)S(1)} %collective-permute-done.3.behind_ref), channel_id=1, source_target_pairs={{0,2},{2,6},{4,0},{6,10},{8,4},{10,14},{12,8},{14,12},{1,3},{3,7},... | collective-permute-start | bytes 368648 | tf_op jit(solution)/shard_map/ppermute | solution.py:175
  14.4 5.7 %collective-permute-start.4 = (bf16[8,7680]{1,0:T(8,128)(2,1)S(1)}, bf16[8,7680]{1,0:T(8,128)(2,1)S(1)}, u32[]{:S(2)}, u32[]{:S(2)}) collective-permute-start(bf16[8,7680]{1,0:T(8,128)(2,1)S(1)} %get-tuple-element.32.token_ref), channel_id=1, source_target_pairs={{8,14},{12,10},{6,0},{2,4},{14,8},{10,12},{0,6},{4,2},{9,15},{13,1... | collective-permute-start | bytes 368648 | tf_op jit(solution)/shard_map/ppermute | solution.py:187
  20.3 4.4 %collective-permute-start.7 = (bf16[80,1536]{1,0:T(8,128)(2,1)S(1)}, bf16[80,1536]{1,0:T(8,128)(2,1)S(1)}, u32[]{:S(2)}, u32[]{:S(2)}) collective-permute-start(bf16[80,1536]{1,0:T(8,128)(2,1)S(1)} %get-tuple-element.37.token_ref.own_ref), channel_id=1, source_target_pairs={{0,1},{1,0},{2,3},{3,2},{4,5},{5,4},{6,7},{7,6},{8,9},{9,8},{10,11... | collective-permute-start | bytes 737288 | tf_op jit(solution)/shard_map/ppermute | solution.py:324

commit v6 on v5

--- a/solution.py
+++ b/solution.py
@@ -11,7 +11,7 @@
 WHOLE = pl.BlockSpec(memory_space=pltpu.VMEM)
 ANYWHERE = pl.BlockSpec(memory_space=pl.ANY)
 IN_HBM = pl.BlockSpec(memory_space=pltpu.HBM)
-SHARES = ([11, 11, 18], 4, 4)
+SHARES = ([11, 11, 19], 3, 4)
 COLS = 1024
 EARLY = 128
 WAITING = 48

time: 37.8 us -> 37.8 us (level)
  transfers between devices with their start and end apart: 8 -> 8, of which waited for: 1 -> 0; matrix products, arithmetic and copies ran while one was open for 0% -> 0% of each run, Pallas kernels for 35% -> 35%
where the time goes in v6:
time: 37.8 us; the launch traced here: 37.5 us
  Pallas kernels  28.8 us (76%)
  starting transfers between devices  8.51 us (23%)
    pallas_call x1, Pallas kernels, update(): pl.pallas_call(functools.partial(update_kernel, columns, per_column), in_...  12.9 us
    pallas_call x3, Pallas kernels, fetch(): pl.pallas_call(functools.partial(fetch_kernel, low), in_specs=[IN_HBM, AN...  8.6 us
    ppermute x6, starting transfers between devices, step(): lax.ppermute(array, axis, [(i, ring[(place[i] + by) % count]) for i in ra...  4.55 us
    pallas_call x1, Pallas kernels, fill(): pl.pallas_call(functools.partial(fill_kernel, low), in_specs=[IN_HBM, ANY...  4.36 us
    pallas_call x1, Pallas kernels, pack(): pl.pallas_call(functools.partial(pack_kernel, packing, low), in_specs=[WH...  2.85 us
    ppermute x1, starting transfers between devices, per_device(): lax.ppermute(own, 'col', [(c, (c + 1) % col_count) for c in range(col_cou...  2.67 us
    ppermute x1, starting transfers between devices, gather_rows(): lax.ppermute(across, axis, [(ring[a], ring[b]) for a, b in pairs])  1.28 us
  transfers between devices with their start and end apart: 8, of which 0 were waited for; matrix products, arithmetic and copies ran while one was open for 0% of the time, Pallas kernels for 35%

profile of v6, /device:TPU:1, one launch (start us, length us, event | category | flops | bytes accessed | tf_op | source)
XLA Modules:
  0.0 37.5 jit_solution(12199320432907545113)
XLA Ops:
  0.0 2.8 %pack.1 = (bf16[8,7680]{1,0:T(8,128)(2,1)S(1)}, f32[608,6144]{1,0:T(8,128)S(1)}) custom-call(bf16[5,6144]{1,0:T(8,128)(2,1)} %first_ref.1, bf16[5,6144]{1,0:T(8,128)(2,1)} %second_ref.1, f32[1536,6144]{1,0:T(8,128)} %schur_hbm.3), custom_call_target="tpu_custom_call" | custom-call | tf_op jit(solution)/shard_map/pack/pallas_call | solution.py:57
  2.9 0.3 collective-permute-start
  3.2 1.2 %collective-permute-start.1 = (bf16[8,7680]{1,0:T(8,128)(2,1)S(1)}, bf16[8,7680]{1,0:T(8,128)(2,1)S(1)}, u32[]{:S(2)}, u32[]{:S(2)}) collective-permute-start(bf16[8,7680]{1,0:T(8,128)(2,1)S(1)} %get-tuple-element.24.token_ref), channel_id=1, source_target_pairs={{0,2},{2,6},{4,0},{6,10},{8,4},{10,14},{12,8},{14,12},{1,3},{3,7},... | collective-permute-start | bytes 368648 | tf_op jit(solution)/shard_map/ppermute | solution.py:175
  4.4 3.5 %fetch.3.refs_0_ = f32[352,6144]{1,0:T(8,128)S(1)} custom-call(f32[1536,6144]{1,0:T(8,128)} %schur_hbm.3, bf16[8,7680]{1,0:T(8,128)(2,1)S(1)} %get-tuple-element.24.token_ref), custom_call_target="tpu_custom_call" | custom-call | bytes 17301504 | tf_op jit(solution)/shard_map/fetch/pallas_call | solution.py:76
  7.8 0.0 collective-permute-done.token_ref
  7.9 0.3 collective-permute-start.2
  8.2 0.0 collective-permute-done.1
  8.2 1.2 %collective-permute-start.3 = (bf16[8,7680]{1,0:T(8,128)(2,1)S(1)}, bf16[8,7680]{1,0:T(8,128)(2,1)S(1)}, u32[]{:S(2)}, u32[]{:S(2)}) collective-permute-start(bf16[8,7680]{1,0:T(8,128)(2,1)S(1)} %collective-permute-done.1), channel_id=1, source_target_pairs={{0,2},{2,6},{4,0},{6,10},{8,4},{10,14},{12,8},{14,12},{1,3},{3,7},... | collective-permute-start | bytes 368648 | tf_op jit(solution)/shard_map/ppermute | solution.py:175
  9.4 3.5 %fetch.4.refs_1_ = f32[352,6144]{1,0:T(8,128)S(1)} custom-call(f32[1536,6144]{1,0:T(8,128)} %schur_hbm.3, bf16[8,7680]{1,0:T(8,128)(2,1)S(1)} %collective-permute-done.token_ref), custom_call_target="tpu_custom_call" | custom-call | bytes 17301504 | tf_op jit(solution)/shard_map/fetch/pallas_call | solution.py:76
  12.9 0.0 collective-permute-done.2.ahead_ref
  12.9 0.3 collective-permute-start.5
  13.2 0.0 collective-permute-done.3.behind_ref
  13.2 1.2 %collective-permute-start.6 = (bf16[8,7680]{1,0:T(8,128)(2,1)S(1)}, bf16[8,7680]{1,0:T(8,128)(2,1)S(1)}, u32[]{:S(2)}, u32[]{:S(2)}) collective-permute-start(bf16[8,7680]{1,0:T(8,128)(2,1)S(1)} %collective-permute-done.3.behind_ref), channel_id=1, source_target_pairs={{0,2},{2,6},{4,0},{6,10},{8,4},{10,14},{12,8},{14,12},{1,3},{3,7},... | collective-permute-start | bytes 368648 | tf_op jit(solution)/shard_map/ppermute | solution.py:175
  14.4 1.3 %collective-permute-start.4 = (bf16[8,7680]{1,0:T(8,128)(2,1)S(1)}, bf16[8,7680]{1,0:T(8,128)(2,1)S(1)}, u32[]{:S(2)}, u32[]{:S(2)}) collective-permute-start(bf16[8,7680]{1,0:T(8,128)(2,1)S(1)} %get-tuple-element.32.token_ref), channel_id=1, source_target_pairs={{8,14},{12,10},{6,0},{2,4},{14,8},{10,12},{0,6},{4,2},{9,15},{13,1... | collective-permute-start | bytes 368648 | tf_op jit(solution)/shard_map/ppermute | solution.py:187
  15.7 4.4 %fill.1.refs_2_ = f32[608,6144]{1,0:T(8,128)S(1)} custom-call(f32[1536,6144]{1,0:T(8,128)} %schur_hbm.3, bf16[8,7680]{1,0:T(8,128)(2,1)S(1)} %get-tuple-element.32.token_ref, f32[608,6144]{1,0:T(8,128)S(1)} %get-tuple-element.33.room_ref), custom_call_target="tpu_custom_call", output_to_operand_aliasing={{}: (2, {})} | custom-call | bytes 29884416 | tf_op jit(solution)/shard_map/fill/pallas_call | solution.py:106
  20.1 0.0 collective-permute-done.5
  20.1 0.0 collective-permute-done.6
  20.1 0.0 collective-permute-done.4
  20.1 0.1 assemble.1
  20.3 2.7 %collective-permute-start.7 = (bf16[80,1536]{1,0:T(8,128)(2,1)S(1)}, bf16[80,1536]{1,0:T(8,128)(2,1)S(1)}, u32[]{:S(2)}, u32[]{:S(2)}) collective-permute-start(bf16[80,1536]{1,0:T(8,128)(2,1)S(1)} %get-tuple-element.37.token_ref.own_ref), channel_id=1, source_target_pairs={{0,1},{1,0},{2,3},{3,2},{4,5},{5,4},{6,7},{7,6},{8,9},{9,8},{10,11... | collective-permute-start | bytes 737288 | tf_op jit(solution)/shard_map/ppermute | solution.py:324
  23.0 1.7 %fetch.5.refs_3_ = f32[96,6144]{1,0:T(8,128)S(1)} custom-call(f32[1536,6144]{1,0:T(8,128)} %schur_hbm.3, bf16[80,1536]{1,0:T(8,128)(2,1)S(1)} %get-tuple-element.37.token_ref.own_ref), custom_call_target="tpu_custom_call" | custom-call | bytes 4718592 | tf_op jit(solution)/shard_map/fetch/pallas_call | solution.py:76
  24.6 0.0 collective-permute-done.7.peer_ref
  24.6 12.9 %update.1 = (f32[1536,6144]{1,0:T(8,128)}, f32[352,6144]{1,0:T(8,128)S(1)}, f32[352,6144]{1,0:T(8,128)S(1)}, f32[608,6144]{1,0:T(8,128)S(1)}, f32[96,6144]{1,0:T(8,128)S(1)}) custom-call(f32[1536,6144]{1,0:T(8,128)} %schur_hbm.3, ...), custom_call_target="tpu_custom_call", output_to_operand_aliasing={{1}: (4, {}), {2}: (5, {}), {3}: (6, {}), {4}: (7, {})} | custom-call | tf_op jit(solution)/shard_map/update/pallas_call | solution.py:293
  (1 shorter events, 0.0 us)
Async XLA Ops:
  2.9 5.0 %collective-permute-start = (bf16[8,7680]{1,0:T(8,128)(2,1)S(1)}, bf16[8,7680]{1,0:T(8,128)(2,1)S(1)}, u32[]{:S(2)}, u32[]{:S(2)}) collective-permute-start(bf16[8,7680]{1,0:T(8,128)(2,1)S(1)} %get-tuple-element.24.token_ref), channel_id=1, source_target_pairs={{0,4},{2,0},{4,8},{6,2},{8,12},{10,6},{12,14},{14,10},{1,5},{3,1},... | collective-permute-start | bytes 368648 | tf_op jit(solution)/shard_map/ppermute | solution.py:175
  3.2 5.0 %collective-permute-start.1 = (bf16[8,7680]{1,0:T(8,128)(2,1)S(1)}, bf16[8,7680]{1,0:T(8,128)(2,1)S(1)}, u32[]{:S(2)}, u32[]{:S(2)}) collective-permute-start(bf16[8,7680]{1,0:T(8,128)(2,1)S(1)} %get-tuple-element.24.token_ref), channel_id=1, source_target_pairs={{0,2},{2,6},{4,0},{6,10},{8,4},{10,14},{12,8},{14,12},{1,3},{3,7},... | collective-permute-start | bytes 368648 | tf_op jit(solution)/shard_map/ppermute | solution.py:175
  7.9 5.0 %collective-permute-start.2 = (bf16[8,7680]{1,0:T(8,128)(2,1)S(1)}, bf16[8,7680]{1,0:T(8,128)(2,1)S(1)}, u32[]{:S(2)}, u32[]{:S(2)}) collective-permute-start(bf16[8,7680]{1,0:T(8,128)(2,1)S(1)} %collective-permute-done.token_ref), channel_id=1, source_target_pairs={{0,4},{2,0},{4,8},{6,2},{8,12},{10,6},{12,14},{14,10},{1,5},{3,1},... | collective-permute-start | bytes 368648 | tf_op jit(solution)/shard_map/ppermute | solution.py:175
  8.2 5.0 %collective-permute-start.3 = (bf16[8,7680]{1,0:T(8,128)(2,1)S(1)}, bf16[8,7680]{1,0:T(8,128)(2,1)S(1)}, u32[]{:S(2)}, u32[]{:S(2)}) collective-permute-start(bf16[8,7680]{1,0:T(8,128)(2,1)S(1)} %collective-permute-done.1), channel_id=1, source_target_pairs={{0,2},{2,6},{4,0},{6,10},{8,4},{10,14},{12,8},{14,12},{1,3},{3,7},... | collective-permute-start | bytes 368648 | tf_op jit(solution)/shard_map/ppermute | solution.py:175
  12.9 7.2 %collective-permute-start.5 = (bf16[8,7680]{1,0:T(8,128)(2,1)S(1)}, bf16[8,7680]{1,0:T(8,128)(2,1)S(1)}, u32[]{:S(2)}, u32[]{:S(2)}) collective-permute-start(bf16[8,7680]{1,0:T(8,128)(2,1)S(1)} %collective-permute-done.2.ahead_ref), channel_id=1, source_target_pairs={{0,4},{2,0},{4,8},{6,2},{8,12},{10,6},{12,14},{14,10},{1,5},{3,1},... | collective-permute-start | bytes 368648 | tf_op jit(solution)/shard_map/ppermute | solution.py:175
  13.2 6.9 %collective-permute-start.6 = (bf16[8,7680]{1,0:T(8,128)(2,1)S(1)}, bf16[8,7680]{1,0:T(8,128)(2,1)S(1)}, u32[]{:S(2)}, u32[]{:S(2)}) collective-permute-start(bf16[8,7680]{1,0:T(8,128)(2,1)S(1)} %collective-permute-done.3.behind_ref), channel_id=1, source_target_pairs={{0,2},{2,6},{4,0},{6,10},{8,4},{10,14},{12,8},{14,12},{1,3},{3,7},... | collective-permute-start | bytes 368648 | tf_op jit(solution)/shard_map/ppermute | solution.py:175
  14.4 5.7 %collective-permute-start.4 = (bf16[8,7680]{1,0:T(8,128)(2,1)S(1)}, bf16[8,7680]{1,0:T(8,128)(2,1)S(1)}, u32[]{:S(2)}, u32[]{:S(2)}) collective-permute-start(bf16[8,7680]{1,0:T(8,128)(2,1)S(1)} %get-tuple-element.32.token_ref), channel_id=1, source_target_pairs={{8,14},{12,10},{6,0},{2,4},{14,8},{10,12},{0,6},{4,2},{9,15},{13,1... | collective-permute-start | bytes 368648 | tf_op jit(solution)/shard_map/ppermute | solution.py:187
  20.3 4.4 %collective-permute-start.7 = (bf16[80,1536]{1,0:T(8,128)(2,1)S(1)}, bf16[80,1536]{1,0:T(8,128)(2,1)S(1)}, u32[]{:S(2)}, u32[]{:S(2)}) collective-permute-start(bf16[80,1536]{1,0:T(8,128)(2,1)S(1)} %get-tuple-element.37.token_ref.own_ref), channel_id=1, source_target_pairs={{0,1},{1,0},{2,3},{3,2},{4,5},{5,4},{6,7},{7,6},{8,9},{9,8},{10,11... | collective-permute-start | bytes 737288 | tf_op jit(solution)/shard_map/ppermute | solution.py:324
